TPU v7x, 256 devices: a whole 4x4x8 slice. The times are simulated.
256 devices in a mesh: seq: 128 (over y, z_hi, x, core), ch: 2 (over z_lo).
Axes of the slice: x: 4, y: 4, z: 8 (z_hi: 4, z_lo: 2; z = z_hi * 2 + z_lo), core: 2. Of those that a mesh axis runs over, the one named last changes fastest.
Arguments:
- query: float32 [8, 1048576], P(None, ('seq', 'ch')), may hold values from -6 to 6
- key: float32 [8, 1048576], P('ch', 'seq'), may hold values from -6 to 6
- value: float32 [8, 1048576], P('ch', 'seq'), may hold values from -6 to 6
- filters: float32 [8, 1048576], P('ch', 'seq'), may hold values from -0.005859375 to 0.005859375
- short_taps: float32 [2, 8, 3], P(None, 'ch'), may hold values from -3.5 to 3.5
- bias: float32 [8], P('ch'), may hold values from -4 to 4
Outputs:
- mixed_out: float32 [8, 1048576], P(None, ('seq', 'ch'))
All inputs are finite; a program needn't handle non-finite values.
Results may differ from a plain program's by a relative error of at most 0.00011.
Values sent between devices are 32-bit elements; how exact they have to be, the bound alone decides.
A program may use at most 64 MiB of HBM per device.

v0:
```python
import functools

import jax
import jax.numpy as jnp
import ml_dtypes
import numpy as np
from jax import lax
from jax.experimental import pallas as pl
from jax.experimental.pallas import tpu as pltpu
from jax.sharding import PartitionSpec as P

MESH = pl.DeviceIdType.MESH
F32 = jnp.float32
BF16 = jnp.bfloat16


def two_parts(table):
    high = table.astype(np.float32).astype(ml_dtypes.bfloat16)
    low = (table - high.astype(np.float64)).astype(np.float32).astype(ml_dtypes.bfloat16)
    return high, low


def as_left(table):
    high, low = two_parts(table)
    return np.concatenate([high, high, low], axis=1)


def as_right(table):
    high, low = two_parts(table)
    return np.concatenate([high, high, low], axis=0)


def make_tables():
    j1, k1 = np.arange(32), np.arange(32)
    lanes = np.arange(128)
    head = 2 * np.pi * np.outer(k1 + 0.5, j1) / 64
    same = np.eye(8)
    step = np.stack([np.cos(head), -np.sin(head)])
    head_in = np.einsum("rkj,ab->rkabj", step, same).reshape(512, 256)
    head_out = np.einsum("rkj,ab->bjrka", step, same).reshape(256, 512)
    turn = np.repeat(2 * np.pi * np.outer(k1 + 0.5, lanes) / 8192, 8, axis=0)
    turn = np.concatenate([np.cos(turn), np.sin(turn)], axis=1).astype(np.float32)
    tail = 2 * np.pi * np.outer(lanes, lanes) / 128
    c, s = np.cos(tail), np.sin(tail)
    tail_in = np.block([[c, -s], [s, c]])
    tail_out = np.block([[c, s], [-s, c]])
    place = np.arange(256).reshape(4, 4, 8, 2).transpose(0, 2, 1, 3).reshape(256)
    nu = np.arange(512)
    phase = 2 * np.pi * np.outer(nu, place) / 512
    block_in = np.concatenate([np.cos(phase), np.sin(phase)], axis=0)
    block_out = []
    for sign in (1, -1):
        wave = np.exp(1j * phase.T) * (1 + sign * 1j * np.exp(-2j * np.pi * nu / 512))[None, :]
        wave = wave * 2.0**-21
        block_out.append(as_left(np.concatenate([wave.real, wave.imag], axis=0)))
    return (
        as_left(head_in),
        as_right(tail_in),
        turn,
        as_left(block_in),
        np.stack(block_out),
        as_right(tail_out),
        as_left(head_out),
    )


def put_split(ref, value, axis):
    high = value.astype(BF16)
    low = (value - high.astype(F32)).astype(BF16)
    n = value.shape[axis]
    for place, part in enumerate((high, low, high)):
        if axis == 0:
            ref[place * n : (place + 1) * n, :] = part
        else:
            ref[:, place * n : (place + 1) * n] = part


def mm(a, b):
    return jnp.dot(a, b, preferred_element_type=F32)


def kernel(
    taps, bias, query, key, value, filt,
    head_in_h, tail_in_h, turn_h, block_in_h, block_out_h, tail_out_h, head_out_h,
    out,
    query_v, key_v, value_v, filt_v,
    head_in, tail_in, turn, block_in, block_out, tail_out, head_out,
    halo, rows, zbuf, sbuf, rbuf, spec, wide, back_s, back_r, done_s, done_r,
    right_a, left_b, right_q, right_i, left_o, right_o,
    load_sem, halo_send, halo_recv, z_send, z_recv, xy_send, xy_recv,
    back_send, back_recv, done_send, done_recv,
):
    seq = lax.axis_index("seq")
    ch = lax.axis_index("ch")
    y = seq // 32
    zh = (seq // 8) % 4
    s = seq % 8
    me = y * 8 + s
    z = zh * 2 + ch

    def xy_device(d):
        return {"seq": (d // 8) * 32 + zh * 8 + d % 8, "ch": ch}

    def z_device(to):
        return {"seq": y * 32 + (to // 2) * 8 + s, "ch": to % 2}

    loads = [
        (filt, filt_v), (key, key_v), (value, value_v),
        (head_in_h, head_in), (turn_h, turn), (tail_in_h, tail_in),
        (block_in_h, block_in), (block_out_h.at[me % 2], block_out),
        (tail_out_h, tail_out), (head_out_h, head_out), (query, query_v),
    ]
    loads = [pltpu.make_async_copy(a, b, load_sem.at[i]) for i, (a, b) in enumerate(loads)]
    for load in loads:
        load.start()
    (l_filt, l_key, l_value, l_hi, l_turn, l_ti, l_bi, l_bo, l_to, l_ho, l_query) = loads

    barrier = pltpu.get_barrier_semaphore()

    @pl.loop(1, 8)
    def _(i):
        pl.semaphore_signal(barrier, inc=1, device_id=z_device((z + i) % 8), device_id_type=MESH)

    pl.semaphore_signal(
        barrier, inc=1, device_id={"seq": (seq + 127) % 128, "ch": ch}, device_id_type=MESH
    )

    @pl.loop(1, 32)
    def _(i):
        pl.semaphore_signal(barrier, inc=1, device_id=xy_device((me + i) % 32), device_id_type=MESH)

    pl.semaphore_wait(barrier, 39)

    halos = [
        pltpu.make_async_remote_copy(
            src_ref=source.at[:, 8064:8192],
            dst_ref=halo.at[i],
            send_sem=halo_send.at[i],
            recv_sem=halo_recv.at[i],
            device_id={"seq": (seq + 1) % 128, "ch": ch},
            device_id_type=MESH,
        )
        for i, source in enumerate((key, value))
    ]
    for copy in halos:
        copy.start()

    def z_exchange(f):
        @pl.loop(1, 4)
        def _(i):
            to = (zh + i) % 4
            pltpu.make_async_remote_copy(
                src_ref=rows.at[f, to],
                dst_ref=zbuf.at[f, zh],
                send_sem=z_send.at[f],
                recv_sem=z_recv.at[f],
                device_id=z_device(to * 2 + ch),
                device_id_type=MESH,
            ).start()

        pltpu.make_async_copy(rows.at[f, zh], zbuf.at[f, zh], z_recv.at[f]).start()

    l_filt.wait()
    rows[0] = filt_v[...].reshape(4, 64, 128)
    first = jnp.where((lax.broadcasted_iota(jnp.int32, (1, 128), 1) == 0) & (seq == 0), 1.0, 0.0)
    for c in range(4):
        rows[0, c, 0:1, :] = rows[0, c, 0:1, :] + first * bias[c]
    z_exchange(0)

    l_key.wait()
    l_value.wait()

    def short(source, i):
        x = source[...]
        t = taps[i]
        return t[:, 0:1] * x + t[:, 1:2] * pltpu.roll(x, 1, 1) + t[:, 2:3] * pltpu.roll(x, 2, 1)

    rows[1] = (short(key_v, 0) * short(value_v, 1)).reshape(4, 64, 128)
    for copy in halos:
        copy.wait_recv()
    lane = lax.broadcasted_iota(jnp.int32, (4, 128), 1)

    def short_first(source, i):
        x = source[:, 0:128]
        t = taps[i]
        before = jnp.where(seq > 0, halo[i], 0.0)
        x1 = jnp.where(lane < 1, pltpu.roll(before, 1, 1), pltpu.roll(x, 1, 1))
        x2 = jnp.where(lane < 2, pltpu.roll(before, 2, 1), pltpu.roll(x, 2, 1))
        return t[:, 0:1] * x + t[:, 1:2] * x1 + t[:, 2:3] * x2

    fixed = short_first(key_v, 0) * short_first(value_v, 1)
    for c in range(4):
        rows[1, c, 0:1, :] = fixed[c : c + 1, :]
    z_exchange(1)

    def forward(f):
        pltpu.make_async_copy(zbuf.at[f], zbuf.at[f], z_recv.at[f]).wait()
        put_split(right_a, zbuf[f].reshape(256, 128), 0)
        if f == 0:
            l_hi.wait()
        real = mm(head_in[0:256, :], right_a[...])
        imag = mm(head_in[256:512, :], right_a[...])
        if f == 0:
            l_turn.wait()
            l_ti.wait()
        c, sn = turn[:, 0:128], turn[:, 128:256]
        turned = jnp.concatenate([real * c + imag * sn, imag * c - real * sn], axis=1)
        put_split(left_b, turned, 1)
        sbuf[f] = mm(left_b[...], tail_in[...]).reshape(32, 8, 256)

        @pl.loop(1, 32)
        def _(i):
            d = (me + i) % 32
            pltpu.make_async_remote_copy(
                src_ref=sbuf.at[f, d],
                dst_ref=rbuf.at[f, me],
                send_sem=xy_send.at[f],
                recv_sem=xy_recv.at[f],
                device_id=xy_device(d),
                device_id_type=MESH,
            ).start()

        pltpu.make_async_copy(sbuf.at[f, me], rbuf.at[f, me], xy_recv.at[f]).start()

    def across(f):
        pltpu.make_async_copy(rbuf.at[f], rbuf.at[f], xy_recv.at[f]).wait()
        put_split(right_q, rbuf[f].reshape(256, 256), 0)
        if f == 0:
            l_bi.wait()
        for m in range(0, 512, 128):
            cosines = mm(block_in[m : m + 128, :], right_q[...])
            sines = mm(block_in[512 + m : 640 + m, :], right_q[...])
            real = cosines[:, 0:128] + sines[:, 128:256]
            imag = cosines[:, 128:256] - sines[:, 0:128]
            if f == 0:
                spec[m : m + 128, 0:128] = real
                spec[m : m + 128, 128:256] = imag
            else:
                freal, fimag = spec[m : m + 128, 0:128], spec[m : m + 128, 128:256]
                prod = jnp.concatenate([real * freal - imag * fimag, real * fimag + imag * freal], axis=1)
                high = prod.astype(BF16)
                low = (prod - high.astype(F32)).astype(BF16)
                right_i[m : m + 128, :] = high
                right_i[512 + m : 640 + m, :] = low
                right_i[1024 + m : 1152 + m, :] = high

    forward(0)
    forward(1)
    across(0)
    across(1)
    l_bo.wait()
    for m in range(0, 256, 128):
        cosines = mm(block_out[m : m + 128, :], right_i[...])
        sines = mm(block_out[256 + m : 384 + m, :], right_i[...])
        real = cosines[:, 0:128] - sines[:, 128:256]
        imag = cosines[:, 128:256] + sines[:, 0:128]
        back_s[m // 8 : m // 8 + 16] = jnp.concatenate([real, imag], axis=1).reshape(16, 8, 256)

    @pl.loop(1, 32)
    def _(i):
        d = (me + i) % 32
        pltpu.make_async_remote_copy(
            src_ref=back_s.at[d],
            dst_ref=back_r.at[me],
            send_sem=back_send,
            recv_sem=back_recv,
            device_id=xy_device(d),
            device_id_type=MESH,
        ).start()

    pltpu.make_async_copy(back_s.at[me], back_r.at[me], back_recv).start()
    pltpu.make_async_copy(back_r, back_r, back_recv).wait()

    put_split(left_o, back_r[...].reshape(256, 256), 1)
    l_to.wait()
    mixed = mm(left_o[...], tail_out[...])
    c, sn = turn[:, 0:128], turn[:, 128:256]
    real, imag = mixed[:, 0:128], mixed[:, 128:256]
    put_split(right_o, jnp.concatenate([real * c - imag * sn, real * sn + imag * c], axis=0), 0)
    l_ho.wait()
    done_s[...] = mm(head_out[...], right_o[...]).reshape(8, 32, 128)

    channel = ch * 4 + zh

    @pl.loop(1, 8)
    def _(i):
        to = (z + i) % 8
        pltpu.make_async_remote_copy(
            src_ref=done_s.at[to],
            dst_ref=done_r.at[channel],
            send_sem=done_send,
            recv_sem=done_recv,
            device_id=z_device(to),
            device_id_type=MESH,
        ).start()

    pltpu.make_async_copy(done_s.at[z], done_r.at[channel], done_recv).start()
    l_query.wait()
    pltpu.make_async_copy(done_r, done_r, done_recv).wait()
    out[...] = done_r[...].reshape(8, 4096) * query_v[...]

    for copy in halos:
        copy.wait_send()
    for f in range(2):
        pltpu.make_async_copy(rows.at[f, 0:3], rows.at[f, 0:3], z_send.at[f]).wait()
        pltpu.make_async_copy(sbuf.at[f, 0:31], sbuf.at[f, 0:31], xy_send.at[f]).wait()
    pltpu.make_async_copy(back_s.at[0:31], back_s.at[0:31], back_send).wait()
    pltpu.make_async_copy(done_s.at[0:7], done_s.at[0:7], done_send).wait()


def local(query, key, value, filters, short_taps, bias):
    tables = make_tables()
    vm = pltpu.VMEM
    dma = pltpu.SemaphoreType.DMA
    any_spec = pl.BlockSpec(memory_space=pl.ANY)
    table_scratch = [vm(t.shape[1:] if t.ndim == 3 else t.shape, t.dtype) for t in tables]
    return pl.pallas_call(
        kernel,
        out_shape=jax.ShapeDtypeStruct((8, 4096), F32),
        in_specs=[
            pl.BlockSpec(memory_space=pltpu.VMEM),
            pl.BlockSpec(memory_space=pltpu.SMEM),
        ]
        + [any_spec] * 11,
        out_specs=pl.BlockSpec(memory_space=pltpu.VMEM),
        scratch_shapes=[vm((8, 4096), F32)]
        + [vm((4, 8192), F32)] * 3
        + table_scratch
        + [
            vm((2, 4, 128), F32),
            vm((2, 4, 64, 128), F32),
            vm((2, 4, 64, 128), F32),
            vm((2, 32, 8, 256), F32),
            vm((2, 32, 8, 256), F32),
            vm((512, 256), F32),
            vm((8, 128), F32),
            vm((32, 8, 256), F32),
            vm((32, 8, 256), F32),
            vm((8, 32, 128), F32),
            vm((8, 32, 128), F32),
            vm((768, 128), BF16),
            vm((256, 768), BF16),
            vm((768, 256), BF16),
            vm((1536, 256), BF16),
            vm((256, 768), BF16),
            vm((1536, 128), BF16),
            dma((11,)),
            dma((2,)), dma((2,)),
            dma((2,)), dma((2,)),
            dma((2,)), dma((2,)),
            dma(()), dma(()),
            dma(()), dma(()),
        ],
        compiler_params=pltpu.CompilerParams(
            collective_id=0, has_side_effects=True, vmem_limit_bytes=56 * 1024 * 1024
        ),
        name="long_convolution",
    )(short_taps, bias, query, key, value, filters, *[jnp.asarray(t) for t in tables])


def solution(mesh):
    return jax.shard_map(
        local,
        mesh=mesh,
        in_specs=(
            P(None, ("seq", "ch")),
            P("ch", "seq"),
            P("ch", "seq"),
            P("ch", "seq"),
            P(None, "ch", None),
            P("ch"),
        ),
        out_specs=P(None, ("seq", "ch")),
        check_vma=False,
    )
```

profile of v0, /device:TPU:1, one launch (start us, length us, event | category | flops | bytes accessed | tf_op | source)
XLA Modules:
  0.0 45.5 jit_solution(883416045677130307)
XLA Ops:
  0.0 1.4 %copy.14.taps = f32[2,4,3]{2,1,0:T(4,128)} copy(f32[2,4,3]{1,0,2:T(2,128)} %param.17) | data formatting | bytes 192 | tf_op args[4]
  1.4 42.6 %long_convolution.1 = f32[8,4096]{1,0:T(8,128)} custom-call(f32[2,4,3]{2,1,0:T(4,128)} %copy.14.taps, f32[4]{0:T(128)} %bias.1, f32[8,4096]{1,0:T(8,128)} %query.1, f32[4,8192]{1,0:T(4,128)} %key.1, f32[4,8192]{1,0:T(4,128)} %value.1, f32[4,8192]{1,0:T(4,128)} %filt.1, bf16[512,768]{1,0:T(8,128)(2,1)} %constant.14.clone.head_in_h, ...), custom_call_target="tpu_custom_call" | custom-call | tf_op jit(solution)/shard_map/long_convolution/pallas_call | solution.py:317
  44.0 1.6 %copy.16 = f32[8,4096]{1,0:T(8,128)} copy(f32[8,4096]{1,0:T(8,128)} %long_convolution.1) | data formatting | bytes 262144
where the time goes:
time: 45.7 us; the launch traced here: 45.5 us
  Pallas kernels  42.6 us (93%)
  local copies, waits for them, and re-layouts  2.93 us (6%)
    pallas_call x1, Pallas kernels, local(): pl.pallas_call(kernel, out_shape=jax.ShapeDtypeStruct((8, 4096), F32), in...  42.6 us
    unnamed x2, local copies, waits for them, and re-layouts  2.93 us

commit v1 on v0

--- a/solution.py
+++ b/solution.py
@@ -80,14 +80,14 @@
 
 
 def kernel(
-    taps, bias, query, key, value, filt,
+    key, value, filt, taps_h, bias_h,
     head_in_h, tail_in_h, turn_h, block_in_h, block_out_h, tail_out_h, head_out_h,
     out,
-    query_v, key_v, value_v, filt_v,
+    key_v, value_v, filt_v, taps, bias,
     head_in, tail_in, turn, block_in, block_out, tail_out, head_out,
-    halo, rows, zbuf, sbuf, rbuf, spec, wide, back_s, back_r, done_s, done_r,
+    gate, ends_s, ends_r, rows_f, rows_s, zbuf_f, zbuf_s, sbuf, rbuf, spec, back_s, back_r, done_s, done_r,
     right_a, left_b, right_q, right_i, left_o, right_o,
-    load_sem, halo_send, halo_recv, z_send, z_recv, xy_send, xy_recv,
+    load_sem, ends_send, ends_recv, z_send, z_recv, xy_send, xy_recv,
     back_send, back_recv, done_send, done_recv,
 ):
     seq = lax.axis_index("seq")
@@ -104,98 +104,136 @@
     def z_device(to):
         return {"seq": y * 32 + (to // 2) * 8 + s, "ch": to % 2}
 
+    barrier = pltpu.get_barrier_semaphore()
+
+    @pl.loop(0, 7)
+    def _(i):
+        pl.semaphore_signal(
+            barrier, inc=1, device_id=z_device((z + 1 + (i + 3) % 7) % 8), device_id_type=MESH
+        )
+
+    @pl.loop(0, 4)
+    def _(i):
+        before = (y * 32 + i * 8 + s + 127) % 128
+        pl.semaphore_signal(barrier, inc=1, device_id={"seq": before, "ch": ch}, device_id_type=MESH)
+
+    @pl.loop(1, 32)
+    def _(i):
+        pl.semaphore_signal(barrier, inc=1, device_id=xy_device((me + i) % 32), device_id_type=MESH)
+
     loads = [
-        (filt, filt_v), (key, key_v), (value, value_v),
+        (filt, filt_v), (bias_h, bias), (key, key_v), (value, value_v), (taps_h, taps),
         (head_in_h, head_in), (turn_h, turn), (tail_in_h, tail_in),
         (block_in_h, block_in), (block_out_h.at[me % 2], block_out),
-        (tail_out_h, tail_out), (head_out_h, head_out), (query, query_v),
+        (tail_out_h, tail_out), (head_out_h, head_out),
     ]
     loads = [pltpu.make_async_copy(a, b, load_sem.at[i]) for i, (a, b) in enumerate(loads)]
     for load in loads:
         load.start()
-    (l_filt, l_key, l_value, l_hi, l_turn, l_ti, l_bi, l_bo, l_to, l_ho, l_query) = loads
-
-    barrier = pltpu.get_barrier_semaphore()
-
-    @pl.loop(1, 8)
-    def _(i):
-        pl.semaphore_signal(barrier, inc=1, device_id=z_device((z + i) % 8), device_id_type=MESH)
-
-    pl.semaphore_signal(
-        barrier, inc=1, device_id={"seq": (seq + 127) % 128, "ch": ch}, device_id_type=MESH
-    )
-
-    @pl.loop(1, 32)
-    def _(i):
-        pl.semaphore_signal(barrier, inc=1, device_id=xy_device((me + i) % 32), device_id_type=MESH)
-
-    pl.semaphore_wait(barrier, 39)
-
-    halos = [
-        pltpu.make_async_remote_copy(
-            src_ref=source.at[:, 8064:8192],
-            dst_ref=halo.at[i],
-            send_sem=halo_send.at[i],
-            recv_sem=halo_recv.at[i],
-            device_id={"seq": (seq + 1) % 128, "ch": ch},
-            device_id_type=MESH,
-        )
-        for i, source in enumerate((key, value))
-    ]
-    for copy in halos:
-        copy.start()
+    drains = []
+    pend = {}
+    (l_filt, l_bias, l_key, l_value, l_taps, l_hi, l_turn, l_ti, l_bi, l_bo, l_to, l_ho) = loads
+
+    l_filt.wait()
+    l_bias.wait()
+    for c in range(4):
+        rows_f[c] = filt_v[pl.ds(c, 64, stride=4), :]
+    first = jnp.where((lax.broadcasted_iota(jnp.int32, (1, 128), 1) == 0) & (seq == 0), 1.0, 0.0)
+    for c in range(4):
+        rows_f[c, 0:1, :] = rows_f[c, 0:1, :] + first * bias[c]
+
+    l_key.wait()
+    l_value.wait()
+    l_taps.wait()
+    for c in range(4):
+        for i, source in enumerate((key_v, value_v)):
+            rows_s[c, 64 + i : 65 + i, :] = source[c : c + 1, :]
+            ends_s[c, i : i + 1, :] = source[252 + c : 253 + c, :]
+
+    pl.semaphore_wait(barrier, 42)
+    zbuf = (zbuf_f, zbuf_s)
+    rows = (rows_f, rows_s)
 
     def z_exchange(f):
         @pl.loop(1, 4)
         def _(i):
-            to = (zh + i) % 4
+            to = (zh + 1 + i % 3) % 4
             pltpu.make_async_remote_copy(
-                src_ref=rows.at[f, to],
-                dst_ref=zbuf.at[f, zh],
+                src_ref=rows[f].at[to],
+                dst_ref=zbuf[f].at[zh],
                 send_sem=z_send.at[f],
                 recv_sem=z_recv.at[f],
                 device_id=z_device(to * 2 + ch),
                 device_id_type=MESH,
             ).start()
 
-        pltpu.make_async_copy(rows.at[f, zh], zbuf.at[f, zh], z_recv.at[f]).start()
-
-    l_filt.wait()
-    rows[0] = filt_v[...].reshape(4, 64, 128)
-    first = jnp.where((lax.broadcasted_iota(jnp.int32, (1, 128), 1) == 0) & (seq == 0), 1.0, 0.0)
-    for c in range(4):
-        rows[0, c, 0:1, :] = rows[0, c, 0:1, :] + first * bias[c]
+        pltpu.make_async_copy(rows[f].at[zh], zbuf[f].at[zh], z_recv.at[f]).start()
+        pend['z',f] = pltpu.make_async_copy(zbuf[f], zbuf[f], z_recv.at[f])
+        drains.append(lambda: pltpu.make_async_copy(rows[f].at[0:3], rows[f].at[0:3], z_send.at[f]).wait())
+
     z_exchange(0)
 
-    l_key.wait()
-    l_value.wait()
+    after = (seq + 1) % 128
+
+    @pl.loop(0, 4)
+    def _(c):
+        pltpu.make_async_remote_copy(
+            src_ref=ends_s.at[c],
+            dst_ref=ends_r.at[(after // 8) % 4],
+            send_sem=ends_send,
+            recv_sem=ends_recv,
+            device_id={"seq": (after // 32) * 32 + c * 8 + after % 8, "ch": ch},
+            device_id_type=MESH,
+        ).start()
+
+    pend['e'] = pltpu.make_async_copy(ends_r, ends_r, ends_recv)
+    drains.append(lambda: pltpu.make_async_copy(ends_s, ends_s, ends_send).wait())
+
+    row = lax.broadcasted_iota(jnp.int32, (8, 128), 0) % 4
+    lanes = lax.broadcasted_iota(jnp.int32, (256, 128), 1)
 
     def short(source, i):
         x = source[...]
-        t = taps[i]
-        return t[:, 0:1] * x + t[:, 1:2] * pltpu.roll(x, 1, 1) + t[:, 2:3] * pltpu.roll(x, 2, 1)
-
-    rows[1] = (short(key_v, 0) * short(value_v, 1)).reshape(4, 64, 128)
-    for copy in halos:
-        copy.wait_recv()
-    lane = lax.broadcasted_iota(jnp.int32, (4, 128), 1)
-
-    def short_first(source, i):
-        x = source[:, 0:128]
-        t = taps[i]
-        before = jnp.where(seq > 0, halo[i], 0.0)
-        x1 = jnp.where(lane < 1, pltpu.roll(before, 1, 1), pltpu.roll(x, 1, 1))
-        x2 = jnp.where(lane < 2, pltpu.roll(before, 2, 1), pltpu.roll(x, 2, 1))
-        return t[:, 0:1] * x + t[:, 1:2] * x1 + t[:, 2:3] * x2
-
-    fixed = short_first(key_v, 0) * short_first(value_v, 1)
+        total = None
+        for j in range(3):
+            t = [taps[j, i, c] for c in range(4)]
+            t = jnp.where(row < 2, jnp.where(row == 0, t[0], t[1]), jnp.where(row == 2, t[2], t[3]))
+            moved = x
+            if j > 0:
+                near = pltpu.roll(x, j, 1)
+                moved = jnp.where(lanes < j, pltpu.roll(near, 4, 0), near)
+            term = t[None] * moved.reshape(32, 8, 128)
+            total = term if total is None else total + term
+        return total
+
+    gate[...] = (short(key_v, 0) * short(value_v, 1)).reshape(256, 128)
     for c in range(4):
-        rows[1, c, 0:1, :] = fixed[c : c + 1, :]
+        rows_s[c, 0:64, :] = gate[pl.ds(c, 64, stride=4), :]
     z_exchange(1)
 
+    def first_rows():
+        pend.pop('e').wait()
+        lane = lax.broadcasted_iota(jnp.int32, (4, 128), 1)
+        origin = lax.broadcasted_iota(jnp.int32, (4, 128), 0) + me == 0
+
+        def whole(i):
+            x = zbuf_s[:, 64 + i, :]
+            before = jnp.where(origin, 0.0, ends_r[:, i, :])
+            total = taps[0, i, zh] * x
+            for j in (1, 2):
+                moved = jnp.where(lane < j, pltpu.roll(before, j, 1), pltpu.roll(x, j, 1))
+                total = total + taps[j, i, zh] * moved
+            return total
+
+        fixed = whole(0) * whole(1)
+        for block in range(4):
+            zbuf_s[block, 0:1, :] = fixed[block : block + 1, :]
+
     def forward(f):
-        pltpu.make_async_copy(zbuf.at[f], zbuf.at[f], z_recv.at[f]).wait()
-        put_split(right_a, zbuf[f].reshape(256, 128), 0)
+        pend.pop(('z',f)).wait()
+        if f == 1:
+            first_rows()
+        put_split(right_a, zbuf[f][:, 0:64, :].reshape(256, 128), 0)
         if f == 0:
             l_hi.wait()
         real = mm(head_in[0:256, :], right_a[...])
@@ -221,9 +259,11 @@
             ).start()
 
         pltpu.make_async_copy(sbuf.at[f, me], rbuf.at[f, me], xy_recv.at[f]).start()
+        pend['x',f] = pltpu.make_async_copy(rbuf.at[f], rbuf.at[f], xy_recv.at[f])
+        drains.append(lambda: pltpu.make_async_copy(sbuf.at[f, 0:31], sbuf.at[f, 0:31], xy_send.at[f]).wait())
 
     def across(f):
-        pltpu.make_async_copy(rbuf.at[f], rbuf.at[f], xy_recv.at[f]).wait()
+        pend.pop(('x',f)).wait()
         put_split(right_q, rbuf[f].reshape(256, 256), 0)
         if f == 0:
             l_bi.wait()
@@ -269,6 +309,7 @@
         ).start()
 
     pltpu.make_async_copy(back_s.at[me], back_r.at[me], back_recv).start()
+    drains.append(lambda: pltpu.make_async_copy(back_s.at[0:31], back_s.at[0:31], back_send).wait())
     pltpu.make_async_copy(back_r, back_r, back_recv).wait()
 
     put_split(left_o, back_r[...].reshape(256, 256), 1)
@@ -278,7 +319,7 @@
     real, imag = mixed[:, 0:128], mixed[:, 128:256]
     put_split(right_o, jnp.concatenate([real * c - imag * sn, real * sn + imag * c], axis=0), 0)
     l_ho.wait()
-    done_s[...] = mm(head_out[...], right_o[...]).reshape(8, 32, 128)
+    done_s[...] = mm(head_out[...], right_o[...])
 
     channel = ch * 4 + zh
 
@@ -286,66 +327,68 @@
     def _(i):
         to = (z + i) % 8
         pltpu.make_async_remote_copy(
-            src_ref=done_s.at[to],
-            dst_ref=done_r.at[channel],
+            src_ref=done_s.at[pl.ds(pl.multiple_of(to * 32, 32), 32)],
+            dst_ref=done_r.at[pl.ds(pl.multiple_of(channel * 32, 32), 32)],
             send_sem=done_send,
             recv_sem=done_recv,
             device_id=z_device(to),
             device_id_type=MESH,
         ).start()
 
-    pltpu.make_async_copy(done_s.at[z], done_r.at[channel], done_recv).start()
-    l_query.wait()
+    pltpu.make_async_copy(
+        done_s.at[pl.ds(pl.multiple_of(z * 32, 32), 32)],
+        done_r.at[pl.ds(pl.multiple_of(channel * 32, 32), 32)],
+        done_recv,
+    ).start()
+    drains.append(lambda: pltpu.make_async_copy(done_s.at[0:224], done_s.at[0:224], done_send).wait())
     pltpu.make_async_copy(done_r, done_r, done_recv).wait()
-    out[...] = done_r[...].reshape(8, 4096) * query_v[...]
-
-    for copy in halos:
-        copy.wait_send()
-    for f in range(2):
-        pltpu.make_async_copy(rows.at[f, 0:3], rows.at[f, 0:3], z_send.at[f]).wait()
-        pltpu.make_async_copy(sbuf.at[f, 0:31], sbuf.at[f, 0:31], xy_send.at[f]).wait()
-    pltpu.make_async_copy(back_s.at[0:31], back_s.at[0:31], back_send).wait()
-    pltpu.make_async_copy(done_s.at[0:7], done_s.at[0:7], done_send).wait()
+    for j in range(32):
+        out[8 * j : 8 * j + 8, :] = done_r[pl.ds(j, 8, stride=32), :]
+
+    for drain in drains:
+        drain()
+
+
+def by_time(x):
+    return x.reshape(4, 64, 128).transpose(1, 0, 2).reshape(256, 128)
 
 
 def local(query, key, value, filters, short_taps, bias):
     tables = make_tables()
     vm = pltpu.VMEM
     dma = pltpu.SemaphoreType.DMA
-    any_spec = pl.BlockSpec(memory_space=pl.ANY)
     table_scratch = [vm(t.shape[1:] if t.ndim == 3 else t.shape, t.dtype) for t in tables]
-    return pl.pallas_call(
+    conv = pl.pallas_call(
         kernel,
-        out_shape=jax.ShapeDtypeStruct((8, 4096), F32),
-        in_specs=[
-            pl.BlockSpec(memory_space=pltpu.VMEM),
-            pl.BlockSpec(memory_space=pltpu.SMEM),
-        ]
-        + [any_spec] * 11,
+        out_shape=jax.ShapeDtypeStruct((256, 128), F32),
+        in_specs=[pl.BlockSpec(memory_space=pl.ANY)] * 12,
         out_specs=pl.BlockSpec(memory_space=pltpu.VMEM),
-        scratch_shapes=[vm((8, 4096), F32)]
-        + [vm((4, 8192), F32)] * 3
+        scratch_shapes=[vm((256, 128), F32)] * 3
+        + [pltpu.SMEM((3, 2, 4), F32), pltpu.SMEM((4,), F32)]
         + table_scratch
         + [
-            vm((2, 4, 128), F32),
-            vm((2, 4, 64, 128), F32),
-            vm((2, 4, 64, 128), F32),
+            vm((256, 128), F32),
+            vm((4, 8, 128), F32),
+            vm((4, 8, 128), F32),
+            vm((4, 64, 128), F32),
+            vm((4, 72, 128), F32),
+            vm((4, 64, 128), F32),
+            vm((4, 72, 128), F32),
             vm((2, 32, 8, 256), F32),
             vm((2, 32, 8, 256), F32),
             vm((512, 256), F32),
-            vm((8, 128), F32),
             vm((32, 8, 256), F32),
             vm((32, 8, 256), F32),
-            vm((8, 32, 128), F32),
-            vm((8, 32, 128), F32),
+            vm((256, 128), F32),
+            vm((256, 128), F32),
             vm((768, 128), BF16),
             vm((256, 768), BF16),
             vm((768, 256), BF16),
             vm((1536, 256), BF16),
             vm((256, 768), BF16),
             vm((1536, 128), BF16),
-            dma((11,)),
-            dma((2,)), dma((2,)),
+            dma((12,)),
+            dma(()), dma(()),
             dma((2,)), dma((2,)),
             dma((2,)), dma((2,)),
             dma(()), dma(()),
@@ -355,7 +398,11 @@
             collective_id=0, has_side_effects=True, vmem_limit_bytes=56 * 1024 * 1024
         ),
         name="long_convolution",
-    )(short_taps, bias, query, key, value, filters, *[jnp.asarray(t) for t in tables])
+    )(
+        by_time(key), by_time(value), by_time(filters), short_taps.transpose(2, 0, 1), bias,
+        *[jnp.asarray(t) for t in tables],
+    )
+    return conv.reshape(32, 8, 128).transpose(1, 0, 2).reshape(8, 4096) * query
 
 
 def solution(mesh):

time: 45.7 us -> 42.8 us (0.937)
  local copies, waits for them, and re-layouts: 2.93 us -> 0.01 us
  other arithmetic: 0 us -> 1.57 us
  Pallas kernels: 42.6 us -> 41.1 us
    unnamed x2, local copies, waits for them, and re-layouts: 2.93 us -> 0.01 us
    mul x0 -> x1, other arithmetic: none -> 1.57 us  [local(): return conv.reshape(32, 8, 128).transpose(1, 0, 2).reshape(8, 4096) * query]
    pallas_call x1, Pallas kernels: 42.6 us -> 41.1 us  [local(): pl.pallas_call(kernel, out_shape=jax.ShapeDtypeStruct((256, 128), F32), i...]
where the time goes in v1:
time: 42.8 us; the launch traced here: 42.7 us
  Pallas kernels  41.1 us (96%)
  other arithmetic  1.57 us (4%)
    pallas_call x1, Pallas kernels, local(): pl.pallas_call(kernel, out_shape=jax.ShapeDtypeStruct((256, 128), F32), i...  41.1 us
    mul x1, other arithmetic, local(): return conv.reshape(32, 8, 128).transpose(1, 0, 2).reshape(8, 4096) * query  1.57 us

profile of v1, /device:TPU:1, one launch (start us, length us, event | category | flops | bytes accessed | tf_op | source)
XLA Modules:
  0.0 42.7 jit_solution(5925371914507622764)
XLA Ops:
  0.0 0.0 copy-start
  0.0 41.1 %long_convolution.1 = f32[256,128]{1,0:T(8,128)} custom-call(f32[256,128]{1,0:T(8,128)} %bitcast.22, f32[256,128]{1,0:T(8,128)} %bitcast.23, f32[256,128]{1,0:T(8,128)} %bitcast.24, f32[3,2,4]{2,1,0:T(2,128)} %bitcast.25, f32[4]{0:T(128)} %bias_h.1, bf16[512,768]{1,0:T(8,128)(2,1)} %constant.14.clone.head_in_h, bf16[768,256]{1,0:T(8,128)(2,1)} %constant.15.clone.tail_in_h, ...), custom_call_target="tpu_custom_call" | custom-call | tf_op jit(solution)/shard_map/long_convolution/pallas_call | solution.py:361
  41.1 0.0 copy-done
  41.1 1.6 %bitcast_multiply_fusion = f32[8,4096]{1,0:T(8,128)} fusion(f32[8,4096]{1,0:T(8,128)S(1)} %copy-done, f32[256,128]{1,0:T(8,128)} %long_convolution.1), kind=kLoop, calls=%fused_computation | loop fusion | flops 32768 | bytes 393216 | tf_op jit(solution)/shard_map/mul | solution.py:405
Async XLA Ops:
  0.0 41.1 %copy-start = (f32[8,4096]{1,0:T(8,128)S(1)}, f32[8,4096]{1,0:T(8,128)}, u32[]{:S(2)}) copy-start(f32[8,4096]{1,0:T(8,128)} %param.13) | copy-start | bytes 393220

commit v2 on v1

v2 whole, which is shorter than its diff:
```python
import functools

import jax
import jax.numpy as jnp
import ml_dtypes
import numpy as np
from jax import lax
from jax.experimental import pallas as pl
from jax.experimental.pallas import tpu as pltpu
from jax.sharding import PartitionSpec as P

MESH = pl.DeviceIdType.MESH
F32 = jnp.float32
BF16 = jnp.bfloat16


def two_parts(table):
    high = table.astype(np.float32).astype(ml_dtypes.bfloat16)
    low = (table - high.astype(np.float64)).astype(np.float32).astype(ml_dtypes.bfloat16)
    return high, low


def as_left(table):
    high, low = two_parts(table)
    return np.concatenate([high, high, low], axis=1)


def as_right(table):
    high, low = two_parts(table)
    return np.concatenate([high, high, low], axis=0)


FORWARD = ((0, 1), (3, 2))
BACK = ((0, 1, 2, 3), (4, 5, 6, 7))


def make_tables():
    j1, k1 = np.arange(32), np.arange(32)
    lanes = np.arange(128)
    head = 2 * np.pi * np.outer(k1 + 0.5, j1) / 64
    same = np.eye(4)
    step = np.stack([np.cos(head), -np.sin(head)])
    head_in = np.einsum("rkj,ab->rkabj", step, same).reshape(256, 128)
    head_out = np.einsum("rkj,ab->bjrka", step, same).reshape(128, 256)
    turn = np.repeat(2 * np.pi * np.outer(k1 + 0.5, lanes) / 8192, 4, axis=0)
    turn = np.concatenate([np.cos(turn), np.sin(turn)], axis=1).astype(np.float32)
    tail = 2 * np.pi * np.outer(lanes, lanes) / 128
    c, s = np.cos(tail), np.sin(tail)
    tail_in = np.block([[c, -s], [s, c]])
    tail_out = np.block([[c, s], [-s, c]])
    place = np.arange(256).reshape(4, 4, 8, 2).transpose(1, 3, 0, 2).reshape(256)
    nu = np.arange(512)
    phase = 2 * np.pi * np.outer(nu, place) / 512
    block_in = np.concatenate([np.cos(phase), np.sin(phase)], axis=0)
    block_out = []
    for sign in (1, -1):
        wave = np.exp(1j * phase.T) * (1 + sign * 1j * np.exp(-2j * np.pi * nu / 512))[None, :]
        wave = wave.reshape(8, 32, 512) * 2.0**-21
        wave = np.stack([wave.real, wave.imag], axis=1).reshape(512, 512)
        block_out.append(as_left(wave))
    return (
        as_left(head_in),
        as_right(tail_in),
        turn,
        as_left(block_in),
        np.stack(block_out),
        as_right(tail_out),
        as_left(head_out),
    )


def put_split(ref, value, axis):
    high = value.astype(BF16)
    low = (value - high.astype(F32)).astype(BF16)
    n = value.shape[axis]
    for place, part in enumerate((high, low, high)):
        if axis == 0:
            ref[place * n : (place + 1) * n, :] = part
        else:
            ref[:, place * n : (place + 1) * n] = part


def mm(a, b):
    return jnp.dot(a, b, preferred_element_type=F32)


def kernel(
    key, value, filt, taps_h, bias_h,
    head_in_h, tail_in_h, turn_h, block_in_h, block_out_h, tail_out_h, head_out_h,
    out,
    key_v, value_v, filt_v, taps, bias,
    head_in, tail_in, turn, block_in, block_out, tail_out, head_out,
    gate, ends_s, ends_z, ends_r, starts, rows_f, rows_s, zbuf_f, zbuf_s, sbuf, rbuf, spec, back_s, back_r, done_s, done_r,
    right_a, left_b, right_q, right_i, left_o, right_o,
    load_sem, ends_send, ends_recv, z_send, z_recv, xy_send, xy_recv,
    back_send, back_recv, done_send, done_recv,
):
    seq = lax.axis_index("seq")
    ch = lax.axis_index("ch")
    y = seq // 32
    zh = (seq // 8) % 4
    s = seq % 8
    me = y * 8 + s
    z = zh * 2 + ch
    zbuf = (zbuf_f, zbuf_s)
    rows = (rows_f, rows_s)

    def xy_device(d):
        return {"seq": (d // 8) * 32 + zh * 8 + d % 8, "ch": ch}

    def z_device(to):
        return {"seq": y * 32 + (to // 2) * 8 + s, "ch": to % 2}

    def tile(i, n=8):
        return pl.ds(pl.multiple_of(i * n, n), n)

    def total(ref, sem):
        return pltpu.make_async_copy(ref, ref, sem)

    barrier = pltpu.get_barrier_semaphore()

    @pl.loop(0, 7)
    def _(i):
        pl.semaphore_signal(
            barrier, inc=1, device_id=z_device((z + 1 + (i + 3) % 7) % 8), device_id_type=MESH
        )

    @pl.loop(1, 32)
    def _(i):
        pl.semaphore_signal(barrier, inc=1, device_id=xy_device((me + i) % 32), device_id_type=MESH)

    loads = [
        (filt, filt_v), (bias_h, bias), (key, key_v), (value, value_v), (taps_h, taps),
        (head_in_h, head_in), (turn_h, turn), (tail_in_h, tail_in),
        (block_in_h, block_in), (block_out_h.at[me % 2], block_out),
        (tail_out_h, tail_out), (head_out_h, head_out),
    ]
    loads = [pltpu.make_async_copy(a, b, load_sem.at[i]) for i, (a, b) in enumerate(loads)]
    for load in loads:
        load.start()
    drains = []
    pend = {}
    (l_filt, l_bias, l_key, l_value, l_taps, l_hi, l_turn, l_ti, l_bi, l_bo, l_to, l_ho) = loads

    l_filt.wait()
    l_bias.wait()
    for c in range(4):
        rows_f[c] = filt_v[pl.ds(c, 64, stride=4), :]
    first = jnp.where((lax.broadcasted_iota(jnp.int32, (1, 128), 1) == 0) & (seq == 0), 1.0, 0.0)
    for c in range(4):
        rows_f[c, 0:1, :] = rows_f[c, 0:1, :] + first * bias[c]

    l_key.wait()
    l_value.wait()
    l_taps.wait()
    for i, source in enumerate((key_v, value_v)):
        for c in range(4):
            ends_s[c, i : i + 1, :] = source[252 + c : 253 + c, :]
            ends_s[c, 2 + i : 3 + i, :] = source[c : c + 1, :]
    row = lax.broadcasted_iota(jnp.int32, (8, 128), 0) % 4
    lanes = lax.broadcasted_iota(jnp.int32, (256, 128), 1)

    def tap_rows(j, i):
        t = [taps[j, i, c] for c in range(4)]
        return jnp.where(row < 2, jnp.where(row == 0, t[0], t[1]), jnp.where(row == 2, t[2], t[3]))

    def short(source, i):
        x = source[...]
        result = None
        for j in range(3):
            t = tap_rows(j, i)
            moved = x
            if j > 0:
                near = pltpu.roll(x, j, 1)
                moved = jnp.where(lanes < j, pltpu.roll(near, 4, 0), near)
            term = t[None] * moved.reshape(32, 8, 128)
            result = term if result is None else result + term
        return result

    gate[...] = (short(key_v, 0) * short(value_v, 1)).reshape(256, 128)
    for c in range(4):
        rows_s[c] = gate[pl.ds(c, 64, stride=4), :]

    pl.semaphore_wait(barrier, 38)

    for i in (2, 3, 1):
        to = (zh + i) % 4
        pltpu.make_async_remote_copy(
            src_ref=ends_s.at[to],
            dst_ref=ends_z.at[zh],
            send_sem=ends_send.at[0],
            recv_sem=ends_recv.at[0],
            device_id=z_device(to * 2 + ch),
            device_id_type=MESH,
        ).start()
    drains.append(total(ends_s.at[0:3], ends_send.at[0]).wait)

    def z_exchange(f):
        for i in (2, 3, 1):
            to = (zh + i) % 4
            pltpu.make_async_remote_copy(
                src_ref=rows[f].at[to],
                dst_ref=zbuf[f].at[4 - i],
                send_sem=z_send.at[f],
                recv_sem=z_recv.at[f, 4 - i],
                device_id=z_device(to * 2 + ch),
                device_id_type=MESH,
            ).start()
            pend['z',f,4-i] = total(zbuf[f].at[4 - i], z_recv.at[f, 4 - i])
        drains.append(lambda: total(rows[f].at[0:3], z_send.at[f]).wait())

    z_exchange(0)
    z_exchange(1)
    ends_z[zh] = ends_s[zh]
    total(ends_z.at[0:3], ends_recv.at[0]).wait()

    @pl.loop(0, 4)
    def _(block):
        after = (y * 32 + block * 8 + s + 1) % 128
        pltpu.make_async_remote_copy(
            src_ref=ends_z.at[block],
            dst_ref=ends_r.at[(after // 8) % 4],
            send_sem=ends_send.at[1],
            recv_sem=ends_recv.at[1],
            device_id={"seq": (after // 32) * 32 + zh * 8 + after % 8, "ch": ch},
            device_id_type=MESH,
        ).start()

    pend['e'] = total(ends_r, ends_recv.at[1])
    drains.append(total(ends_z, ends_send.at[1]).wait)

    def first_rows():
        pend.pop('e').wait()
        lane = lax.broadcasted_iota(jnp.int32, (4, 128), 1)
        origin = lax.broadcasted_iota(jnp.int32, (4, 128), 0) + me == 0

        def whole(i):
            x = jnp.concatenate([ends_z[b, 2 + i : 3 + i, :] for b in range(4)], axis=0)
            before = jnp.concatenate([ends_r[b, i : i + 1, :] for b in range(4)], axis=0)
            before = jnp.where(origin, 0.0, before)
            result = taps[0, i, zh] * x
            for j in (1, 2):
                moved = jnp.where(lane < j, pltpu.roll(before, j, 1), pltpu.roll(x, j, 1))
                result = result + taps[j, i, zh] * moved
            return result

        fixed = whole(0) * whole(1)
        for b in range(4):
            starts[b, 0:1, :] = fixed[b : b + 1, :]

    for f in range(2):
        zbuf[f][0] = rows[f][zh]

    def forward(f, p):
        for d in FORWARD[p]:
            if d != 0:
                pend.pop(('z',f,d)).wait()
        if f == 1:
            if p == 0:
                first_rows()
            for d in FORWARD[p]:
                zbuf_s[d, 0:1, :] = starts[(zh + d) % 4, 0:1, :]
        put_split(right_a, jnp.concatenate([zbuf[f][d] for d in FORWARD[p]], axis=0), 0)
        if f == 0 and p == 0:
            l_hi.wait()
        real = mm(head_in[0:128, :], right_a[...])
        imag = mm(head_in[128:256, :], right_a[...])
        if f == 0 and p == 0:
            l_turn.wait()
            l_ti.wait()
        c, sn = turn[:, 0:128], turn[:, 128:256]
        turned = jnp.concatenate([real * c + imag * sn, imag * c - real * sn], axis=1)
        put_split(left_b, turned, 1)
        spread = mm(left_b[...], tail_in[...])
        sbuf[f, p, pl.ds(0, 128, stride=2), :] = spread[:, 0:128]
        sbuf[f, p, pl.ds(1, 128, stride=2), :] = spread[:, 128:256]

        @pl.loop(1, 32)
        def _(i):
            d = (me + i) % 32
            pltpu.make_async_remote_copy(
                src_ref=sbuf.at[f, p, tile(d)],
                dst_ref=rbuf.at[f, p, tile(me)],
                send_sem=xy_send.at[f, p],
                recv_sem=xy_recv.at[f, p],
                device_id=xy_device(d),
                device_id_type=MESH,
            ).start()

        rbuf[f, p, tile(me), :] = sbuf[f, p, tile(me), :]
        pend['x',f,p] = total(rbuf.at[f, p, 0:248], xy_recv.at[f, p])
        drains.append(lambda: total(sbuf.at[f, p, 0:248], xy_send.at[f, p]).wait())

    def across(f):
        for p in range(2):
            pend.pop(('x',f,p)).wait()
            for n, d in enumerate(FORWARD[p]):
                for half in range(2):
                    at = n * 4 + half * 2
                    pair = [rbuf[f, p, pl.ds(at + i, 32, stride=8), :] for i in range(2)]
                    pair = jnp.concatenate(pair, axis=1)
                    high = pair.astype(BF16)
                    low = (pair - high.astype(F32)).astype(BF16)
                    base = (zh + d) % 4 * 64 + half * 32
                    for k, part in enumerate((high, low, high)):
                        right_q[pl.ds(pl.multiple_of(base + 256 * k, 32), 32), :] = part
        if f == 0:
            l_bi.wait()
        for m in range(0, 512, 128):
            cosines = mm(block_in[m : m + 128, :], right_q[...])
            sines = mm(block_in[512 + m : 640 + m, :], right_q[...])
            real = cosines[:, 0:128] + sines[:, 128:256]
            imag = cosines[:, 128:256] - sines[:, 0:128]
            if f == 0:
                spec[m : m + 128, 0:128] = real
                spec[m : m + 128, 128:256] = imag
            else:
                freal, fimag = spec[m : m + 128, 0:128], spec[m : m + 128, 128:256]
                prod = jnp.concatenate([real * freal - imag * fimag, real * fimag + imag * freal], axis=1)
                high = prod.astype(BF16)
                low = (prod - high.astype(F32)).astype(BF16)
                right_i[m : m + 128, :] = high
                right_i[512 + m : 640 + m, :] = low
                right_i[1024 + m : 1152 + m, :] = high

    forward(0, 0)
    forward(0, 1)
    forward(1, 0)
    forward(1, 1)
    across(0)
    across(1)
    l_bo.wait()

    def send_back(p):
        both = mm(block_out[256 * p : 256 * p + 256, :], right_i[...])
        for n in range(4):
            cosines, sines = both[64 * n : 64 * n + 32], both[64 * n + 32 : 64 * n + 64]
            real = cosines[:, 0:128] - sines[:, 128:256]
            imag = cosines[:, 128:256] + sines[:, 0:128]
            back_s[p, pl.ds(2 * n, 32, stride=8), :] = real
            back_s[p, pl.ds(2 * n + 1, 32, stride=8), :] = imag

        @pl.loop(1, 32)
        def _(i):
            d = (me + i) % 32
            pltpu.make_async_remote_copy(
                src_ref=back_s.at[p, tile(d)],
                dst_ref=back_r.at[p, tile(me)],
                send_sem=back_send.at[p],
                recv_sem=back_recv.at[p],
                device_id=xy_device(d),
                device_id_type=MESH,
            ).start()

        back_r[p, tile(me), :] = back_s[p, tile(me), :]
        pend['b',p] = total(back_r.at[p, 0:248], back_recv.at[p])
        drains.append(lambda: total(back_s.at[p, 0:248], back_send.at[p]).wait())

    send_back(0)
    send_back(1)
    channel = ch * 4 + zh

    def finish_blocks(p):
        pend.pop(('b',p)).wait()
        pair = [back_r[p, pl.ds(i, 128, stride=2), :] for i in range(2)]
        put_split(left_o, jnp.concatenate(pair, axis=1), 1)
        if p == 0:
            l_to.wait()
            l_ho.wait()
        mixed = mm(left_o[...], tail_out[...])
        c, sn = turn[:, 0:128], turn[:, 128:256]
        real, imag = mixed[:, 0:128], mixed[:, 128:256]
        put_split(right_o, jnp.concatenate([real * c - imag * sn, real * sn + imag * c], axis=0), 0)
        done_s[128 * p : 128 * p + 128, :] = mm(head_out[...], right_o[...])

        @pl.loop(4 * p, 4 * p + 4)
        def _(to):
            @pl.when(to == z)
            def _():
                done_r[tile(channel, 32), :] = done_s[tile(to, 32), :]

            @pl.when(to != z)
            def _():
                pltpu.make_async_remote_copy(
                    src_ref=done_s.at[tile(to, 32)],
                    dst_ref=done_r.at[tile(channel, 32)],
                    send_sem=done_send,
                    recv_sem=done_recv,
                    device_id=z_device(to),
                    device_id_type=MESH,
                ).start()

    finish_blocks(0)
    finish_blocks(1)
    total(done_r.at[0:224], done_recv).wait()
    for j in range(32):
        out[8 * j : 8 * j + 8, :] = done_r[pl.ds(j, 8, stride=32), :]
    total(done_s.at[0:224], done_send).wait()
    for drain in drains:
        drain()


def by_time(x):
    return x.reshape(4, 64, 128).transpose(1, 0, 2).reshape(256, 128)


def local(query, key, value, filters, short_taps, bias):
    tables = make_tables()
    vm = pltpu.VMEM
    dma = pltpu.SemaphoreType.DMA
    table_scratch = [vm(t.shape if t.ndim == 2 else (512, 1536), t.dtype) for t in tables]
    conv = pl.pallas_call(
        kernel,
        out_shape=jax.ShapeDtypeStruct((256, 128), F32),
        in_specs=[pl.BlockSpec(memory_space=pl.ANY)] * 12,
        out_specs=pl.BlockSpec(memory_space=pltpu.VMEM),
        scratch_shapes=[vm((256, 128), F32)] * 3
        + [pltpu.SMEM((3, 2, 4), F32), pltpu.SMEM((4,), F32)]
        + table_scratch
        + [
            vm((256, 128), F32),
            vm((4, 8, 128), F32),
            vm((4, 8, 128), F32),
            vm((4, 8, 128), F32),
            vm((4, 8, 128), F32),
            vm((4, 64, 128), F32),
            vm((4, 64, 128), F32),
            vm((4, 64, 128), F32),
            vm((4, 64, 128), F32),
            vm((2, 2, 256, 128), F32),
            vm((2, 2, 256, 128), F32),
            vm((512, 256), F32),
            vm((2, 256, 128), F32),
            vm((2, 256, 128), F32),
            vm((256, 128), F32),
            vm((256, 128), F32),
            vm((384, 128), BF16),
            vm((128, 768), BF16),
            vm((768, 256), BF16),
            vm((1536, 256), BF16),
            vm((128, 768), BF16),
            vm((768, 128), BF16),
            dma((12,)),
            dma((2,)), dma((2,)),
            dma((2,)), dma((2, 4)),
            dma((2, 2)), dma((2, 2)),
            dma((2,)), dma((2,)),
            dma(()), dma(()),
        ],
        compiler_params=pltpu.CompilerParams(
            collective_id=0, has_side_effects=True, vmem_limit_bytes=56 * 1024 * 1024
        ),
        name="long_convolution",
    )(
        by_time(key), by_time(value), by_time(filters), short_taps.transpose(2, 0, 1), bias,
        *[jnp.asarray(t) for t in tables],
    )
    return conv.reshape(32, 8, 128).transpose(1, 0, 2).reshape(8, 4096) * query


def solution(mesh):
    return jax.shard_map(
        local,
        mesh=mesh,
        in_specs=(
            P(None, ("seq", "ch")),
            P("ch", "seq"),
            P("ch", "seq"),
            P("ch", "seq"),
            P(None, "ch", None),
            P("ch"),
        ),
        out_specs=P(None, ("seq", "ch")),
        check_vma=False,
    )
```

time: 42.8 us -> 41.3 us (0.965)
  Pallas kernels: 41.1 us -> 39.6 us
    pallas_call x1, Pallas kernels: 41.1 us -> 39.6 us  [local(): pl.pallas_call(kernel, out_shape=jax.ShapeDtypeStruct((256, 128), F32), i...]
where the time goes in v2:
time: 41.3 us; the launch traced here: 41.2 us
  Pallas kernels  39.6 us (96%)
  other arithmetic  1.57 us (4%)
    pallas_call x1, Pallas kernels, local(): pl.pallas_call(kernel, out_shape=jax.ShapeDtypeStruct((256, 128), F32), i...  39.6 us
    mul x1, other arithmetic, local(): return conv.reshape(32, 8, 128).transpose(1, 0, 2).reshape(8, 4096) * query  1.57 us

profile of v2, /device:TPU:1, one launch (start us, length us, event | category | flops | bytes accessed | tf_op | source)
XLA Modules:
  0.0 41.2 jit_solution(6637455098425105672)
XLA Ops:
  0.0 0.0 copy-start
  0.0 39.6 %long_convolution.1 = f32[256,128]{1,0:T(8,128)} custom-call(f32[256,128]{1,0:T(8,128)} %bitcast.22, f32[256,128]{1,0:T(8,128)} %bitcast.23, f32[256,128]{1,0:T(8,128)} %bitcast.24, f32[3,2,4]{2,1,0:T(2,128)} %bitcast.25, f32[4]{0:T(128)} %bias_h.1, bf16[256,384]{1,0:T(8,128)(2,1)} %constant.14.clone.head_in_h, bf16[768,256]{1,0:T(8,128)(2,1)} %constant.15.clone.tail_in_h, ...), custom_call_target="tpu_custom_call" | custom-call | tf_op jit(solution)/shard_map/long_convolution/pallas_call | solution.py:412
  39.6 0.0 copy-done
  39.6 1.6 %bitcast_multiply_fusion = f32[8,4096]{1,0:T(8,128)} fusion(f32[8,4096]{1,0:T(8,128)S(1)} %copy-done, f32[256,128]{1,0:T(8,128)} %long_convolution.1), kind=kLoop, calls=%fused_computation | loop fusion | flops 32768 | bytes 393216 | tf_op jit(solution)/shard_map/mul | solution.py:458
Async XLA Ops:
  0.0 39.6 %copy-start = (f32[8,4096]{1,0:T(8,128)S(1)}, f32[8,4096]{1,0:T(8,128)}, u32[]{:S(2)}) copy-start(f32[8,4096]{1,0:T(8,128)} %param.13) | copy-start | bytes 393220

commit v3 on v2

--- a/solution.py
+++ b/solution.py
@@ -31,19 +31,23 @@
 
 
 FORWARD = ((0, 1), (3, 2))
-BACK = ((0, 1, 2, 3), (4, 5, 6, 7))
+BACK = ((0, 1), (2, 3), (4, 5, 6, 7))
+PLANE = sorted(
+    ((a, b, e) for a in range(4) for b in range(4) for e in range(2) if (a, b, e) != (0, 0, 0)),
+    key=lambda p: (-(2 - abs(2 - p[0])) - (2 - abs(2 - p[1])), p),
+)
 
 
 def make_tables():
     j1, k1 = np.arange(32), np.arange(32)
     lanes = np.arange(128)
     head = 2 * np.pi * np.outer(k1 + 0.5, j1) / 64
-    same = np.eye(4)
     step = np.stack([np.cos(head), -np.sin(head)])
-    head_in = np.einsum("rkj,ab->rkabj", step, same).reshape(256, 128)
-    head_out = np.einsum("rkj,ab->bjrka", step, same).reshape(128, 256)
-    turn = np.repeat(2 * np.pi * np.outer(k1 + 0.5, lanes) / 8192, 4, axis=0)
-    turn = np.concatenate([np.cos(turn), np.sin(turn)], axis=1).astype(np.float32)
+    head_in = np.einsum("rkj,ab->rakbj", step, np.eye(4)).reshape(256, 128)
+    head_out = [np.einsum("rkj,ab->bjrak", step, np.eye(n)).reshape(32 * n, 64 * n) for n in (2, 4)]
+    angle = 2 * np.pi * np.outer(k1 + 0.5, lanes) / 8192
+    turn = np.concatenate([np.cos(angle), np.sin(angle)], axis=1).astype(np.float32)
+    turn = [np.tile(turn, (n, 1)) for n in (2, 4)]
     tail = 2 * np.pi * np.outer(lanes, lanes) / 128
     c, s = np.cos(tail), np.sin(tail)
     tail_in = np.block([[c, -s], [s, c]])
@@ -61,11 +65,13 @@
     return (
         as_left(head_in),
         as_right(tail_in),
-        turn,
+        turn[0],
+        turn[1],
         as_left(block_in),
         np.stack(block_out),
         as_right(tail_out),
-        as_left(head_out),
+        as_left(head_out[0]),
+        as_left(head_out[1]),
     )
 
 
@@ -86,10 +92,10 @@
 
 def kernel(
     key, value, filt, taps_h, bias_h,
-    head_in_h, tail_in_h, turn_h, block_in_h, block_out_h, tail_out_h, head_out_h,
+    head_in_h, tail_in_h, turn2_h, turn4_h, block_in_h, block_out_h, tail_out_h, head_out2_h, head_out4_h,
     out,
     key_v, value_v, filt_v, taps, bias,
-    head_in, tail_in, turn, block_in, block_out, tail_out, head_out,
+    head_in, tail_in, turn2, turn4, block_in, block_out, tail_out, head_out2, head_out4,
     gate, ends_s, ends_z, ends_r, starts, rows_f, rows_s, zbuf_f, zbuf_s, sbuf, rbuf, spec, back_s, back_r, done_s, done_r,
     right_a, left_b, right_q, right_i, left_o, right_o,
     load_sem, ends_send, ends_recv, z_send, z_recv, xy_send, xy_recv,
@@ -105,8 +111,14 @@
     zbuf = (zbuf_f, zbuf_s)
     rows = (rows_f, rows_s)
 
-    def xy_device(d):
-        return {"seq": (d // 8) * 32 + zh * 8 + d % 8, "ch": ch}
+    in_y = [(y + a) % 4 for a in range(4)]
+    in_x = [(s // 2 + b) % 4 * 2 for b in range(4)]
+    in_core = [s % 2, 1 - s % 2]
+
+    def plane_peers():
+        for a, b, e in PLANE:
+            at = in_x[b] + in_core[e]
+            yield in_y[a] * 8 + at, {"seq": in_y[a] * 32 + zh * 8 + at, "ch": ch}
 
     def z_device(to):
         return {"seq": y * 32 + (to // 2) * 8 + s, "ch": to % 2}
@@ -125,22 +137,21 @@
             barrier, inc=1, device_id=z_device((z + 1 + (i + 3) % 7) % 8), device_id_type=MESH
         )
 
-    @pl.loop(1, 32)
-    def _(i):
-        pl.semaphore_signal(barrier, inc=1, device_id=xy_device((me + i) % 32), device_id_type=MESH)
+    for _, peer in plane_peers():
+        pl.semaphore_signal(barrier, inc=1, device_id=peer, device_id_type=MESH)
 
     loads = [
         (filt, filt_v), (bias_h, bias), (key, key_v), (value, value_v), (taps_h, taps),
-        (head_in_h, head_in), (turn_h, turn), (tail_in_h, tail_in),
+        (head_in_h, head_in), (turn4_h, turn4), (tail_in_h, tail_in),
         (block_in_h, block_in), (block_out_h.at[me % 2], block_out),
-        (tail_out_h, tail_out), (head_out_h, head_out),
+        (tail_out_h, tail_out), (turn2_h, turn2), (head_out2_h, head_out2), (head_out4_h, head_out4),
     ]
     loads = [pltpu.make_async_copy(a, b, load_sem.at[i]) for i, (a, b) in enumerate(loads)]
     for load in loads:
         load.start()
     drains = []
     pend = {}
-    (l_filt, l_bias, l_key, l_value, l_taps, l_hi, l_turn, l_ti, l_bi, l_bo, l_to, l_ho) = loads
+    (l_filt, l_bias, l_key, l_value, l_taps, l_hi, l_turn, l_ti, l_bi, l_bo, l_to, l_t2, l_ho2, l_ho4) = loads
 
     l_filt.wait()
     l_bias.wait()
@@ -268,28 +279,25 @@
         if f == 0 and p == 0:
             l_turn.wait()
             l_ti.wait()
-        c, sn = turn[:, 0:128], turn[:, 128:256]
+        c, sn = turn4[:, 0:128], turn4[:, 128:256]
         turned = jnp.concatenate([real * c + imag * sn, imag * c - real * sn], axis=1)
         put_split(left_b, turned, 1)
         spread = mm(left_b[...], tail_in[...])
-        sbuf[f, p, pl.ds(0, 128, stride=2), :] = spread[:, 0:128]
-        sbuf[f, p, pl.ds(1, 128, stride=2), :] = spread[:, 128:256]
-
-        @pl.loop(1, 32)
-        def _(i):
-            d = (me + i) % 32
+        for b in range(4):
+            for i in range(2):
+                sbuf[f, p, :, 2 * b + i, :] = spread[32 * b : 32 * b + 32, 128 * i : 128 * i + 128]
+        for d, peer in plane_peers():
             pltpu.make_async_remote_copy(
-                src_ref=sbuf.at[f, p, tile(d)],
-                dst_ref=rbuf.at[f, p, tile(me)],
+                src_ref=sbuf.at[f, p, d],
+                dst_ref=rbuf.at[f, p, me],
                 send_sem=xy_send.at[f, p],
                 recv_sem=xy_recv.at[f, p],
-                device_id=xy_device(d),
+                device_id=peer,
                 device_id_type=MESH,
             ).start()
-
-        rbuf[f, p, tile(me), :] = sbuf[f, p, tile(me), :]
-        pend['x',f,p] = total(rbuf.at[f, p, 0:248], xy_recv.at[f, p])
-        drains.append(lambda: total(sbuf.at[f, p, 0:248], xy_send.at[f, p]).wait())
+        rbuf[f, p, me] = sbuf[f, p, me]
+        pend['x',f,p] = total(rbuf.at[f, p, 0:31], xy_recv.at[f, p])
+        drains.append(lambda: total(sbuf.at[f, p, 0:31], xy_send.at[f, p]).wait())
 
     def across(f):
         for p in range(2):
@@ -297,7 +305,7 @@
             for n, d in enumerate(FORWARD[p]):
                 for half in range(2):
                     at = n * 4 + half * 2
-                    pair = [rbuf[f, p, pl.ds(at + i, 32, stride=8), :] for i in range(2)]
+                    pair = [rbuf[f, p, :, at + i, :] for i in range(2)]
                     pair = jnp.concatenate(pair, axis=1)
                     high = pair.astype(BF16)
                     low = (pair - high.astype(F32)).astype(BF16)
@@ -332,57 +340,64 @@
     l_bo.wait()
 
     def send_back(p):
-        both = mm(block_out[256 * p : 256 * p + 256, :], right_i[...])
-        for n in range(4):
+        low, count = 64 * BACK[p][0], len(BACK[p])
+        both = mm(block_out[low : low + 64 * count, :], right_i[...])
+        for n in range(count):
             cosines, sines = both[64 * n : 64 * n + 32], both[64 * n + 32 : 64 * n + 64]
-            real = cosines[:, 0:128] - sines[:, 128:256]
-            imag = cosines[:, 128:256] + sines[:, 0:128]
-            back_s[p, pl.ds(2 * n, 32, stride=8), :] = real
-            back_s[p, pl.ds(2 * n + 1, 32, stride=8), :] = imag
-
-        @pl.loop(1, 32)
-        def _(i):
-            d = (me + i) % 32
+            back_s[p][:, 2 * n, :] = cosines[:, 0:128] - sines[:, 128:256]
+            back_s[p][:, 2 * n + 1, :] = cosines[:, 128:256] + sines[:, 0:128]
+        for d, peer in plane_peers():
             pltpu.make_async_remote_copy(
-                src_ref=back_s.at[p, tile(d)],
-                dst_ref=back_r.at[p, tile(me)],
+                src_ref=back_s[p].at[d],
+                dst_ref=back_r[p].at[me],
                 send_sem=back_send.at[p],
                 recv_sem=back_recv.at[p],
-                device_id=xy_device(d),
+                device_id=peer,
                 device_id_type=MESH,
             ).start()
-
-        back_r[p, tile(me), :] = back_s[p, tile(me), :]
-        pend['b',p] = total(back_r.at[p, 0:248], back_recv.at[p])
-        drains.append(lambda: total(back_s.at[p, 0:248], back_send.at[p]).wait())
-
-    send_back(0)
-    send_back(1)
+        back_r[p][me] = back_s[p][me]
+        pend['b',p] = total(back_r[p].at[0:31], back_recv.at[p])
+        drains.append(lambda: total(back_s[p].at[0:31], back_send.at[p]).wait())
+
+    for p in range(len(BACK)):
+        send_back(p)
     channel = ch * 4 + zh
 
     def finish_blocks(p):
+        count = len(BACK[p])
+        turn, head_out = (turn2, head_out2) if count == 2 else (turn4, head_out4)
         pend.pop(('b',p)).wait()
-        pair = [back_r[p, pl.ds(i, 128, stride=2), :] for i in range(2)]
-        put_split(left_o, jnp.concatenate(pair, axis=1), 1)
+        high_low = []
+        for i in range(2):
+            for n in range(count):
+                part = back_r[p][:, 2 * n + i, :]
+                high = part.astype(BF16)
+                low = (part - high.astype(F32)).astype(BF16)
+                for k, piece in enumerate((high, low, high)):
+                    left_o[32 * n : 32 * n + 32, 256 * k + 128 * i : 256 * k + 128 * i + 128] = piece
         if p == 0:
             l_to.wait()
-            l_ho.wait()
-        mixed = mm(left_o[...], tail_out[...])
+            l_t2.wait()
+            l_ho2.wait()
+            l_ho4.wait()
+        mixed = mm(left_o[0 : 32 * count, :], tail_out[...])
         c, sn = turn[:, 0:128], turn[:, 128:256]
         real, imag = mixed[:, 0:128], mixed[:, 128:256]
-        put_split(right_o, jnp.concatenate([real * c - imag * sn, real * sn + imag * c], axis=0), 0)
-        done_s[128 * p : 128 * p + 128, :] = mm(head_out[...], right_o[...])
-
-        @pl.loop(4 * p, 4 * p + 4)
-        def _(to):
+        right = right_o.at[0 : 192 * count]
+        put_split(right, jnp.concatenate([real * c - imag * sn, real * sn + imag * c], axis=0), 0)
+        low = 32 * BACK[p][0]
+        done_s[low : low + 32 * count, :] = mm(head_out[...], right[...])
+        for to in BACK[p]:
+            block = done_s.at[32 * to : 32 * to + 32]
+
             @pl.when(to == z)
             def _():
-                done_r[tile(channel, 32), :] = done_s[tile(to, 32), :]
+                done_r[tile(channel, 32), :] = block[...]
 
             @pl.when(to != z)
             def _():
                 pltpu.make_async_remote_copy(
-                    src_ref=done_s.at[tile(to, 32)],
+                    src_ref=block,
                     dst_ref=done_r.at[tile(channel, 32)],
                     send_sem=done_send,
                     recv_sem=done_recv,
@@ -390,8 +405,8 @@
                     device_id_type=MESH,
                 ).start()
 
-    finish_blocks(0)
-    finish_blocks(1)
+    for p in range(len(BACK)):
+        finish_blocks(p)
     total(done_r.at[0:224], done_recv).wait()
     for j in range(32):
         out[8 * j : 8 * j + 8, :] = done_r[pl.ds(j, 8, stride=32), :]
@@ -412,7 +427,7 @@
     conv = pl.pallas_call(
         kernel,
         out_shape=jax.ShapeDtypeStruct((256, 128), F32),
-        in_specs=[pl.BlockSpec(memory_space=pl.ANY)] * 12,
+        in_specs=[pl.BlockSpec(memory_space=pl.ANY)] * 14,
         out_specs=pl.BlockSpec(memory_space=pltpu.VMEM),
         scratch_shapes=[vm((256, 128), F32)] * 3
         + [pltpu.SMEM((3, 2, 4), F32), pltpu.SMEM((4,), F32)]
@@ -427,11 +442,11 @@
             vm((4, 64, 128), F32),
             vm((4, 64, 128), F32),
             vm((4, 64, 128), F32),
-            vm((2, 2, 256, 128), F32),
-            vm((2, 2, 256, 128), F32),
+            vm((2, 2, 32, 8, 128), F32),
+            vm((2, 2, 32, 8, 128), F32),
             vm((512, 256), F32),
-            vm((2, 256, 128), F32),
-            vm((2, 256, 128), F32),
+            [vm((32, 2 * len(p), 128), F32) for p in BACK],
+            [vm((32, 2 * len(p), 128), F32) for p in BACK],
             vm((256, 128), F32),
             vm((256, 128), F32),
             vm((384, 128), BF16),
@@ -440,11 +455,11 @@
             vm((1536, 256), BF16),
             vm((128, 768), BF16),
             vm((768, 128), BF16),
-            dma((12,)),
+            dma((14,)),
             dma((2,)), dma((2,)),
             dma((2,)), dma((2, 4)),
             dma((2, 2)), dma((2, 2)),
-            dma((2,)), dma((2,)),
+            dma((3,)), dma((3,)),
             dma(()), dma(()),
         ],
         compiler_params=pltpu.CompilerParams(

time: 41.3 us -> 39.3 us (0.952)
  Pallas kernels: 39.6 us -> 37.6 us
    pallas_call x1, Pallas kernels: 39.6 us -> 37.6 us  [local(): pl.pallas_call(kernel, out_shape=jax.ShapeDtypeStruct((256, 128), F32), i...]
where the time goes in v3:
time: 39.3 us; the launch traced here: 39.2 us
  Pallas kernels  37.6 us (96%)
  other arithmetic  1.57 us (4%)
    pallas_call x1, Pallas kernels, local(): pl.pallas_call(kernel, out_shape=jax.ShapeDtypeStruct((256, 128), F32), i...  37.6 us
    mul x1, other arithmetic, local(): return conv.reshape(32, 8, 128).transpose(1, 0, 2).reshape(8, 4096) * query  1.57 us

profile of v3, /device:TPU:1, one launch (start us, length us, event | category | flops | bytes accessed | tf_op | source)
XLA Modules:
  0.0 39.2 jit_solution(1950709568614302543)
XLA Ops:
  0.0 0.0 copy-start
  0.0 37.6 %long_convolution.1 = f32[256,128]{1,0:T(8,128)} custom-call(f32[256,128]{1,0:T(8,128)} %bitcast.22, f32[256,128]{1,0:T(8,128)} %bitcast.23, f32[256,128]{1,0:T(8,128)} %bitcast.24, f32[3,2,4]{2,1,0:T(2,128)} %bitcast.25, f32[4]{0:T(128)} %bias_h.1, bf16[256,384]{1,0:T(8,128)(2,1)} %constant.18.clone.head_in_h, bf16[768,256]{1,0:T(8,128)(2,1)} %constant.19.clone.tail_in_h, ...), custom_call_target="tpu_custom_call" | custom-call | tf_op jit(solution)/shard_map/long_convolution/pallas_call | solution.py:427
  37.7 0.0 copy-done
  37.7 1.6 %bitcast_multiply_fusion = f32[8,4096]{1,0:T(8,128)} fusion(f32[8,4096]{1,0:T(8,128)S(1)} %copy-done, f32[256,128]{1,0:T(8,128)} %long_convolution.1), kind=kLoop, calls=%fused_computation | loop fusion | flops 32768 | bytes 393216 | tf_op jit(solution)/shard_map/mul | solution.py:473
Async XLA Ops:
  0.0 37.7 %copy-start = (f32[8,4096]{1,0:T(8,128)S(1)}, f32[8,4096]{1,0:T(8,128)}, u32[]{:S(2)}) copy-start(f32[8,4096]{1,0:T(8,128)} %param.15) | copy-start | bytes 393220

commit v4 on v3

--- a/solution.py
+++ b/solution.py
@@ -30,7 +30,10 @@
     return np.concatenate([high, high, low], axis=0)
 
 
-FORWARD = ((0, 1), (3, 2))
+FORWARD = (
+    (((0, 0), (0, 1)), ((1, 0), (1, 1), (3, 0), (3, 1)), ((2, 0), (2, 1))),
+    (((0, 1), (2, 1)), ((0, 0), (2, 0)), ((1, 0), (1, 1), (3, 0), (3, 1))),
+)
 BACK = ((0, 1), (2, 3), (4, 5, 6, 7))
 PLANE = sorted(
     ((a, b, e) for a in range(4) for b in range(4) for e in range(2) if (a, b, e) != (0, 0, 0)),
@@ -38,12 +41,15 @@
 )
 
 
+NEAR = [p for p in PLANE if p[:2] in ((0, 0), (0, 1), (0, 3), (1, 0), (3, 0))]
+
+
 def make_tables():
     j1, k1 = np.arange(32), np.arange(32)
     lanes = np.arange(128)
     head = 2 * np.pi * np.outer(k1 + 0.5, j1) / 64
     step = np.stack([np.cos(head), -np.sin(head)])
-    head_in = np.einsum("rkj,ab->rakbj", step, np.eye(4)).reshape(256, 128)
+    head_in = [np.einsum("rkj,ab->rakbj", step, np.eye(n)).reshape(64 * n, 32 * n) for n in (2, 4)]
     head_out = [np.einsum("rkj,ab->bjrak", step, np.eye(n)).reshape(32 * n, 64 * n) for n in (2, 4)]
     angle = 2 * np.pi * np.outer(k1 + 0.5, lanes) / 8192
     turn = np.concatenate([np.cos(angle), np.sin(angle)], axis=1).astype(np.float32)
@@ -63,7 +69,8 @@
         wave = np.stack([wave.real, wave.imag], axis=1).reshape(512, 512)
         block_out.append(as_left(wave))
     return (
-        as_left(head_in),
+        as_left(head_in[0]),
+        as_left(head_in[1]),
         as_right(tail_in),
         turn[0],
         turn[1],
@@ -92,14 +99,14 @@
 
 def kernel(
     key, value, filt, taps_h, bias_h,
-    head_in_h, tail_in_h, turn2_h, turn4_h, block_in_h, block_out_h, tail_out_h, head_out2_h, head_out4_h,
+    head_in2_h, head_in4_h, tail_in_h, turn2_h, turn4_h, block_in_h, block_out_h, tail_out_h, head_out2_h, head_out4_h,
     out,
     key_v, value_v, filt_v, taps, bias,
-    head_in, tail_in, turn2, turn4, block_in, block_out, tail_out, head_out2, head_out4,
+    head_in2, head_in4, tail_in, turn2, turn4, block_in, block_out, tail_out, head_out2, head_out4,
     gate, ends_s, ends_z, ends_r, starts, rows_f, rows_s, zbuf_f, zbuf_s, sbuf, rbuf, spec, back_s, back_r, done_s, done_r,
     right_a, left_b, right_q, right_i, left_o, right_o,
     load_sem, ends_send, ends_recv, z_send, z_recv, xy_send, xy_recv,
-    back_send, back_recv, done_send, done_recv,
+    back_send, back_recv, done_send, done_recv, widen,
 ):
     seq = lax.axis_index("seq")
     ch = lax.axis_index("ch")
@@ -115,8 +122,8 @@
     in_x = [(s // 2 + b) % 4 * 2 for b in range(4)]
     in_core = [s % 2, 1 - s % 2]
 
-    def plane_peers():
-        for a, b, e in PLANE:
+    def plane_peers(places=PLANE):
+        for a, b, e in places:
             at = in_x[b] + in_core[e]
             yield in_y[a] * 8 + at, {"seq": in_y[a] * 32 + zh * 8 + at, "ch": ch}
 
@@ -137,21 +144,21 @@
             barrier, inc=1, device_id=z_device((z + 1 + (i + 3) % 7) % 8), device_id_type=MESH
         )
 
-    for _, peer in plane_peers():
+    for _, peer in plane_peers(NEAR):
         pl.semaphore_signal(barrier, inc=1, device_id=peer, device_id_type=MESH)
 
     loads = [
         (filt, filt_v), (bias_h, bias), (key, key_v), (value, value_v), (taps_h, taps),
-        (head_in_h, head_in), (turn4_h, turn4), (tail_in_h, tail_in),
+        (head_in4_h, head_in4), (turn4_h, turn4), (tail_in_h, tail_in),
         (block_in_h, block_in), (block_out_h.at[me % 2], block_out),
-        (tail_out_h, tail_out), (turn2_h, turn2), (head_out2_h, head_out2), (head_out4_h, head_out4),
+        (tail_out_h, tail_out), (turn2_h, turn2), (head_in2_h, head_in2), (head_out2_h, head_out2), (head_out4_h, head_out4),
     ]
     loads = [pltpu.make_async_copy(a, b, load_sem.at[i]) for i, (a, b) in enumerate(loads)]
     for load in loads:
         load.start()
     drains = []
     pend = {}
-    (l_filt, l_bias, l_key, l_value, l_taps, l_hi, l_turn, l_ti, l_bi, l_bo, l_to, l_t2, l_ho2, l_ho4) = loads
+    (l_filt, l_bias, l_key, l_value, l_taps, l_hi, l_turn, l_ti, l_bi, l_bo, l_to, l_t2, l_hi2, l_ho2, l_ho4) = loads
 
     l_filt.wait()
     l_bias.wait()
@@ -192,7 +199,7 @@
     for c in range(4):
         rows_s[c] = gate[pl.ds(c, 64, stride=4), :]
 
-    pl.semaphore_wait(barrier, 38)
+    pl.semaphore_wait(barrier, 16)
 
     for i in (2, 3, 1):
         to = (zh + i) % 4
@@ -222,6 +229,10 @@
 
     z_exchange(0)
     z_exchange(1)
+    for k in range(3):
+        for _, peer in plane_peers(NEAR):
+            pl.semaphore_signal(widen.at[k], inc=1, device_id=peer, device_id_type=MESH)
+        pl.semaphore_wait(widen.at[k], 9)
     ends_z[zh] = ends_s[zh]
     total(ends_z.at[0:3], ends_recv.at[0]).wait()
 
@@ -263,55 +274,58 @@
         zbuf[f][0] = rows[f][zh]
 
     def forward(f, p):
-        for d in FORWARD[p]:
-            if d != 0:
+        which = FORWARD[f][p]
+        count = len(which)
+        head_in, turn = (head_in2, turn2) if count == 2 else (head_in4, turn4)
+        for d, half in which:
+            if ('z', f, d) in pend:
                 pend.pop(('z',f,d)).wait()
-        if f == 1:
-            if p == 0:
-                first_rows()
-            for d in FORWARD[p]:
+            if f == 1 and half == 0:
+                if 'e' in pend:
+                    first_rows()
                 zbuf_s[d, 0:1, :] = starts[(zh + d) % 4, 0:1, :]
-        put_split(right_a, jnp.concatenate([zbuf[f][d] for d in FORWARD[p]], axis=0), 0)
+        blocks = [zbuf[f][d, 32 * half : 32 * half + 32, :] for d, half in which]
+        right = right_a.at[0 : 96 * count]
+        put_split(right, jnp.concatenate(blocks, axis=0), 0)
+        if f == 0 and p == 1:
+            l_hi.wait()
+            l_turn.wait()
+        real = mm(head_in[0 : 32 * count, :], right[...])
+        imag = mm(head_in[32 * count : 64 * count, :], right[...])
         if f == 0 and p == 0:
-            l_hi.wait()
-        real = mm(head_in[0:128, :], right_a[...])
-        imag = mm(head_in[128:256, :], right_a[...])
-        if f == 0 and p == 0:
-            l_turn.wait()
             l_ti.wait()
-        c, sn = turn4[:, 0:128], turn4[:, 128:256]
+        c, sn = turn[:, 0:128], turn[:, 128:256]
         turned = jnp.concatenate([real * c + imag * sn, imag * c - real * sn], axis=1)
-        put_split(left_b, turned, 1)
-        spread = mm(left_b[...], tail_in[...])
-        for b in range(4):
+        left = left_b.at[0 : 32 * count]
+        put_split(left, turned, 1)
+        spread = mm(left[...], tail_in[...])
+        for b in range(count):
             for i in range(2):
-                sbuf[f, p, :, 2 * b + i, :] = spread[32 * b : 32 * b + 32, 128 * i : 128 * i + 128]
+                sbuf[f][p][:, 2 * b + i, :] = spread[32 * b : 32 * b + 32, 128 * i : 128 * i + 128]
         for d, peer in plane_peers():
             pltpu.make_async_remote_copy(
-                src_ref=sbuf.at[f, p, d],
-                dst_ref=rbuf.at[f, p, me],
+                src_ref=sbuf[f][p].at[d],
+                dst_ref=rbuf[f][p].at[me],
                 send_sem=xy_send.at[f, p],
                 recv_sem=xy_recv.at[f, p],
                 device_id=peer,
                 device_id_type=MESH,
             ).start()
-        rbuf[f, p, me] = sbuf[f, p, me]
-        pend['x',f,p] = total(rbuf.at[f, p, 0:31], xy_recv.at[f, p])
-        drains.append(lambda: total(sbuf.at[f, p, 0:31], xy_send.at[f, p]).wait())
+        rbuf[f][p][me] = sbuf[f][p][me]
+        pend['x',f,p] = total(rbuf[f][p].at[0:31], xy_recv.at[f, p])
+        drains.append(lambda: total(sbuf[f][p].at[0:31], xy_send.at[f, p]).wait())
 
     def across(f):
-        for p in range(2):
+        for p in range(len(FORWARD[f])):
             pend.pop(('x',f,p)).wait()
-            for n, d in enumerate(FORWARD[p]):
-                for half in range(2):
-                    at = n * 4 + half * 2
-                    pair = [rbuf[f, p, :, at + i, :] for i in range(2)]
-                    pair = jnp.concatenate(pair, axis=1)
-                    high = pair.astype(BF16)
-                    low = (pair - high.astype(F32)).astype(BF16)
-                    base = (zh + d) % 4 * 64 + half * 32
-                    for k, part in enumerate((high, low, high)):
-                        right_q[pl.ds(pl.multiple_of(base + 256 * k, 32), 32), :] = part
+            for n, (d, half) in enumerate(FORWARD[f][p]):
+                pair = [rbuf[f][p][:, 2 * n + i, :] for i in range(2)]
+                pair = jnp.concatenate(pair, axis=1)
+                high = pair.astype(BF16)
+                low = (pair - high.astype(F32)).astype(BF16)
+                base = (zh + d) % 4 * 64 + half * 32
+                for k, part in enumerate((high, low, high)):
+                    right_q[pl.ds(pl.multiple_of(base + 256 * k, 32), 32), :] = part
         if f == 0:
             l_bi.wait()
         for m in range(0, 512, 128):
@@ -331,10 +345,11 @@
                 right_i[512 + m : 640 + m, :] = low
                 right_i[1024 + m : 1152 + m, :] = high
 
-    forward(0, 0)
-    forward(0, 1)
-    forward(1, 0)
-    forward(1, 1)
+    l_t2.wait()
+    l_hi2.wait()
+    for f in range(2):
+        for p in range(len(FORWARD[f])):
+            forward(f, p)
     across(0)
     across(1)
     l_bo.wait()
@@ -377,7 +392,6 @@
                     left_o[32 * n : 32 * n + 32, 256 * k + 128 * i : 256 * k + 128 * i + 128] = piece
         if p == 0:
             l_to.wait()
-            l_t2.wait()
             l_ho2.wait()
             l_ho4.wait()
         mixed = mm(left_o[0 : 32 * count, :], tail_out[...])
@@ -427,7 +441,7 @@
     conv = pl.pallas_call(
         kernel,
         out_shape=jax.ShapeDtypeStruct((256, 128), F32),
-        in_specs=[pl.BlockSpec(memory_space=pl.ANY)] * 14,
+        in_specs=[pl.BlockSpec(memory_space=pl.ANY)] * 15,
         out_specs=pl.BlockSpec(memory_space=pltpu.VMEM),
         scratch_shapes=[vm((256, 128), F32)] * 3
         + [pltpu.SMEM((3, 2, 4), F32), pltpu.SMEM((4,), F32)]
@@ -442,8 +456,8 @@
             vm((4, 64, 128), F32),
             vm((4, 64, 128), F32),
             vm((4, 64, 128), F32),
-            vm((2, 2, 32, 8, 128), F32),
-            vm((2, 2, 32, 8, 128), F32),
+            [[vm((32, 2 * len(p), 128), F32) for p in pieces] for pieces in FORWARD],
+            [[vm((32, 2 * len(p), 128), F32) for p in pieces] for pieces in FORWARD],
             vm((512, 256), F32),
             [vm((32, 2 * len(p), 128), F32) for p in BACK],
             [vm((32, 2 * len(p), 128), F32) for p in BACK],
@@ -455,12 +469,13 @@
             vm((1536, 256), BF16),
             vm((128, 768), BF16),
             vm((768, 128), BF16),
-            dma((14,)),
+            dma((15,)),
             dma((2,)), dma((2,)),
             dma((2,)), dma((2, 4)),
-            dma((2, 2)), dma((2, 2)),
+            dma((2, 3)), dma((2, 3)),
             dma((3,)), dma((3,)),
             dma(()), dma(()),
+            pltpu.SemaphoreType.REGULAR((3,)),
         ],
         compiler_params=pltpu.CompilerParams(
             collective_id=0, has_side_effects=True, vmem_limit_bytes=56 * 1024 * 1024

time: 39.3 us -> 38.7 us (0.985)
  Pallas kernels: 37.6 us -> 37 us
    pallas_call x1, Pallas kernels: 37.6 us -> 37 us  [local(): pl.pallas_call(kernel, out_shape=jax.ShapeDtypeStruct((256, 128), F32), i...]
where the time goes in v4:
time: 38.7 us; the launch traced here: 38.6 us
  Pallas kernels  37 us (96%)
  other arithmetic  1.57 us (4%)
    pallas_call x1, Pallas kernels, local(): pl.pallas_call(kernel, out_shape=jax.ShapeDtypeStruct((256, 128), F32), i...  37 us
    mul x1, other arithmetic, local(): return conv.reshape(32, 8, 128).transpose(1, 0, 2).reshape(8, 4096) * query  1.57 us

profile of v4, /device:TPU:1, one launch (start us, length us, event | category | flops | bytes accessed | tf_op | source)
XLA Modules:
  0.0 38.6 jit_solution(4151982472894680640)
XLA Ops:
  0.0 0.0 copy-start
  0.0 37.0 %long_convolution.1 = f32[256,128]{1,0:T(8,128)} custom-call(f32[256,128]{1,0:T(8,128)} %bitcast.22, f32[256,128]{1,0:T(8,128)} %bitcast.23, f32[256,128]{1,0:T(8,128)} %bitcast.24, f32[3,2,4]{2,1,0:T(2,128)} %bitcast.25, f32[4]{0:T(128)} %bias_h.1, bf16[128,192]{1,0:T(8,128)(2,1)} %constant.20.clone.head_in2_h, bf16[256,384]{1,0:T(8,128)(2,1)} %constant.21.clone.head_in4_h, ...), custom_call_target="tpu_custom_call" | custom-call | tf_op jit(solution)/shard_map/long_convolution/pallas_call | solution.py:441
  37.0 0.0 copy-done
  37.0 1.6 %bitcast_multiply_fusion = f32[8,4096]{1,0:T(8,128)} fusion(f32[8,4096]{1,0:T(8,128)S(1)} %copy-done, f32[256,128]{1,0:T(8,128)} %long_convolution.1), kind=kLoop, calls=%fused_computation | loop fusion | flops 32768 | bytes 393216 | tf_op jit(solution)/shard_map/mul | solution.py:488
Async XLA Ops:
  0.0 37.0 %copy-start = (f32[8,4096]{1,0:T(8,128)S(1)}, f32[8,4096]{1,0:T(8,128)}, u32[]{:S(2)}) copy-start(f32[8,4096]{1,0:T(8,128)} %param.16) | copy-start | bytes 393220

commit v5 on v4

--- a/solution.py
+++ b/solution.py
@@ -59,15 +59,15 @@
     tail_in = np.block([[c, -s], [s, c]])
     tail_out = np.block([[c, s], [-s, c]])
     place = np.arange(256).reshape(4, 4, 8, 2).transpose(1, 3, 0, 2).reshape(256)
-    nu = np.arange(512)
+    nu = np.arange(256)
     phase = 2 * np.pi * np.outer(nu, place) / 512
-    block_in = np.concatenate([np.cos(phase), np.sin(phase)], axis=0)
-    block_out = []
-    for sign in (1, -1):
-        wave = np.exp(1j * phase.T) * (1 + sign * 1j * np.exp(-2j * np.pi * nu / 512))[None, :]
-        wave = wave.reshape(8, 32, 512) * 2.0**-21
-        wave = np.stack([wave.real, wave.imag], axis=1).reshape(512, 512)
-        block_out.append(as_left(wave))
+    cosines, sines = np.cos(phase), np.sin(phase)
+    sines[0] = np.cos(np.pi * place)
+    block_in = np.concatenate([cosines, sines], axis=0)
+    block_out = block_in.T * 2.0**-21
+    shift = np.stack([np.sin(2 * np.pi * nu / 512), np.cos(2 * np.pi * nu / 512), np.cos(2 * np.pi * nu / 512)])
+    shift[2, 0] = -1.0
+    shift = np.repeat(shift, 128, axis=0).T.astype(np.float32)
     return (
         as_left(head_in[0]),
         as_left(head_in[1]),
@@ -75,7 +75,8 @@
         turn[0],
         turn[1],
         as_left(block_in),
-        np.stack(block_out),
+        as_left(block_out),
+        shift,
         as_right(tail_out),
         as_left(head_out[0]),
         as_left(head_out[1]),
@@ -99,11 +100,11 @@
 
 def kernel(
     key, value, filt, taps_h, bias_h,
-    head_in2_h, head_in4_h, tail_in_h, turn2_h, turn4_h, block_in_h, block_out_h, tail_out_h, head_out2_h, head_out4_h,
+    head_in2_h, head_in4_h, tail_in_h, turn2_h, turn4_h, block_in_h, block_out_h, shift_h, tail_out_h, head_out2_h, head_out4_h,
     out,
     key_v, value_v, filt_v, taps, bias,
-    head_in2, head_in4, tail_in, turn2, turn4, block_in, block_out, tail_out, head_out2, head_out4,
-    gate, ends_s, ends_z, ends_r, starts, rows_f, rows_s, zbuf_f, zbuf_s, sbuf, rbuf, spec, back_s, back_r, done_s, done_r,
+    head_in2, head_in4, tail_in, turn2, turn4, block_in, block_out, shift, tail_out, head_out2, head_out4,
+    gate, ends_s, ends_z, ends_r, starts, rows_f, rows_s, zbuf_f, zbuf_s, sbuf, rbuf, spec, back_s, back_r, done_s,
     right_a, left_b, right_q, right_i, left_o, right_o,
     load_sem, ends_send, ends_recv, z_send, z_recv, xy_send, xy_recv,
     back_send, back_recv, done_send, done_recv, widen,
@@ -150,7 +151,7 @@
     loads = [
         (filt, filt_v), (bias_h, bias), (key, key_v), (value, value_v), (taps_h, taps),
         (head_in4_h, head_in4), (turn4_h, turn4), (tail_in_h, tail_in),
-        (block_in_h, block_in), (block_out_h.at[me % 2], block_out),
+        (block_in_h, block_in), (shift_h, shift), (block_out_h, block_out),
         (tail_out_h, tail_out), (turn2_h, turn2), (head_in2_h, head_in2), (head_out2_h, head_out2), (head_out4_h, head_out4),
     ]
     loads = [pltpu.make_async_copy(a, b, load_sem.at[i]) for i, (a, b) in enumerate(loads)]
@@ -158,7 +159,7 @@
         load.start()
     drains = []
     pend = {}
-    (l_filt, l_bias, l_key, l_value, l_taps, l_hi, l_turn, l_ti, l_bi, l_bo, l_to, l_t2, l_hi2, l_ho2, l_ho4) = loads
+    (l_filt, l_bias, l_key, l_value, l_taps, l_hi, l_turn, l_ti, l_bi, l_sh, l_bo, l_to, l_t2, l_hi2, l_ho2, l_ho4) = loads
 
     l_filt.wait()
     l_bias.wait()
@@ -315,6 +316,12 @@
         pend['x',f,p] = total(rbuf[f][p].at[0:31], xy_recv.at[f, p])
         drains.append(lambda: total(sbuf[f][p].at[0:31], xy_send.at[f, p]).wait())
 
+    top_row = lax.broadcasted_iota(jnp.int32, (128, 128), 0) == 0
+    sign = jnp.where(me % 2 == 0, 1.0, -1.0)
+
+    def times(a, b):
+        return a[0] * b[0] - a[1] * b[1], a[0] * b[1] + a[1] * b[0]
+
     def across(f):
         for p in range(len(FORWARD[f])):
             pend.pop(('x',f,p)).wait()
@@ -328,22 +335,35 @@
                     right_q[pl.ds(pl.multiple_of(base + 256 * k, 32), 32), :] = part
         if f == 0:
             l_bi.wait()
-        for m in range(0, 512, 128):
-            cosines = mm(block_in[m : m + 128, :], right_q[...])
-            sines = mm(block_in[512 + m : 640 + m, :], right_q[...])
-            real = cosines[:, 0:128] + sines[:, 128:256]
-            imag = cosines[:, 128:256] - sines[:, 0:128]
+            l_sh.wait()
+        for m in range(0, 256, 128):
+            part = slice(m, m + 128)
+            cosines = mm(block_in[part, :], right_q[...])
+            sines = mm(block_in[256 + m : 384 + m, :], right_q[...])
+            cre, cim, sre, sim = cosines[:, 0:128], cosines[:, 128:256], sines[:, 0:128], sines[:, 128:256]
+
+            def alone(first, other):
+                return jnp.where(top_row, first, other) if m == 0 else other
+
+            up = alone(cre, cre + sim), alone(cim, cim - sre)
+            down = alone(sre, cre - sim), alone(sim, cim + sre)
             if f == 0:
-                spec[m : m + 128, 0:128] = real
-                spec[m : m + 128, 128:256] = imag
+                tilt = sign * shift[part, 0:128]
+                up = times(up, (1.0 + tilt, sign * shift[part, 128:256]))
+                down = times(down, (1.0 - tilt, sign * shift[part, 256:384]))
+                for k, x in enumerate(up + down):
+                    spec[part, 128 * k : 128 * k + 128] = x
             else:
-                freal, fimag = spec[m : m + 128, 0:128], spec[m : m + 128, 128:256]
-                prod = jnp.concatenate([real * freal - imag * fimag, real * fimag + imag * freal], axis=1)
-                high = prod.astype(BF16)
-                low = (prod - high.astype(F32)).astype(BF16)
-                right_i[m : m + 128, :] = high
-                right_i[512 + m : 640 + m, :] = low
-                right_i[1024 + m : 1152 + m, :] = high
+                up = times(up, (spec[part, 0:128], spec[part, 128:256]))
+                down = times(down, (spec[part, 256:384], spec[part, 384:512]))
+                even = [alone(up[k], up[k] + down[k]) for k in range(2)]
+                odd = [alone(down[0], down[1] - up[1]), alone(down[1], up[0] - down[0])]
+                for at, pair in ((m, even), (256 + m, odd)):
+                    pair = jnp.concatenate(pair, axis=1)
+                    high = pair.astype(BF16)
+                    low = (pair - high.astype(F32)).astype(BF16)
+                    for k, x in enumerate((high, low, high)):
+                        right_i[512 * k + at : 512 * k + at + 128, :] = x
 
     l_t2.wait()
     l_hi2.wait()
@@ -355,12 +375,11 @@
     l_bo.wait()
 
     def send_back(p):
-        low, count = 64 * BACK[p][0], len(BACK[p])
-        both = mm(block_out[low : low + 64 * count, :], right_i[...])
+        low, count = 32 * BACK[p][0], len(BACK[p])
+        both = mm(block_out[low : low + 32 * count, :], right_i[...])
         for n in range(count):
-            cosines, sines = both[64 * n : 64 * n + 32], both[64 * n + 32 : 64 * n + 64]
-            back_s[p][:, 2 * n, :] = cosines[:, 0:128] - sines[:, 128:256]
-            back_s[p][:, 2 * n + 1, :] = cosines[:, 128:256] + sines[:, 0:128]
+            for i in range(2):
+                back_s[p][:, 2 * n + i, :] = both[32 * n : 32 * n + 32, 128 * i : 128 * i + 128]
         for d, peer in plane_peers():
             pltpu.make_async_remote_copy(
                 src_ref=back_s[p].at[d],
@@ -406,13 +425,13 @@
 
             @pl.when(to == z)
             def _():
-                done_r[tile(channel, 32), :] = block[...]
+                pltpu.make_async_copy(block, out.at[tile(channel, 32)], done_recv).start()
 
             @pl.when(to != z)
             def _():
                 pltpu.make_async_remote_copy(
                     src_ref=block,
-                    dst_ref=done_r.at[tile(channel, 32)],
+                    dst_ref=out.at[tile(channel, 32)],
                     send_sem=done_send,
                     recv_sem=done_recv,
                     device_id=z_device(to),
@@ -421,12 +440,32 @@
 
     for p in range(len(BACK)):
         finish_blocks(p)
-    total(done_r.at[0:224], done_recv).wait()
-    for j in range(32):
-        out[8 * j : 8 * j + 8, :] = done_r[pl.ds(j, 8, stride=32), :]
+    total(out, done_recv).wait()
     total(done_s.at[0:224], done_send).wait()
     for drain in drains:
         drain()
+
+
+def mix(conv, query, out, conv_v, query_v, out_v, sem):
+    loads, stores = [], []
+    for k in range(4):
+        lanes = pl.ds(1024 * k, 1024)
+        loads.append((
+            pltpu.make_async_copy(conv.at[:, 8 * k : 8 * k + 8], conv_v.at[k], sem.at[0, k]),
+            pltpu.make_async_copy(query.at[:, lanes], query_v.at[:, lanes], sem.at[1, k]),
+        ))
+        stores.append(pltpu.make_async_copy(out_v.at[:, lanes], out.at[:, lanes], sem.at[2, k]))
+        for load in loads[k]:
+            load.start()
+    for k in range(4):
+        for load in loads[k]:
+            load.wait()
+        for j in range(8):
+            lanes = slice(1024 * k + 128 * j, 1024 * k + 128 * j + 128)
+            out_v[:, lanes] = conv_v[k, :, j, :] * query_v[:, lanes]
+        stores[k].start()
+    for store in stores:
+        store.wait()
 
 
 def by_time(x):
@@ -437,12 +476,12 @@
     tables = make_tables()
     vm = pltpu.VMEM
     dma = pltpu.SemaphoreType.DMA
-    table_scratch = [vm(t.shape if t.ndim == 2 else (512, 1536), t.dtype) for t in tables]
+    table_scratch = [vm(t.shape, t.dtype) for t in tables]
     conv = pl.pallas_call(
         kernel,
         out_shape=jax.ShapeDtypeStruct((256, 128), F32),
-        in_specs=[pl.BlockSpec(memory_space=pl.ANY)] * 15,
-        out_specs=pl.BlockSpec(memory_space=pltpu.VMEM),
+        in_specs=[pl.BlockSpec(memory_space=pl.ANY)] * 16,
+        out_specs=pl.BlockSpec(memory_space=pl.ANY),
         scratch_shapes=[vm((256, 128), F32)] * 3
         + [pltpu.SMEM((3, 2, 4), F32), pltpu.SMEM((4,), F32)]
         + table_scratch
@@ -458,10 +497,9 @@
             vm((4, 64, 128), F32),
             [[vm((32, 2 * len(p), 128), F32) for p in pieces] for pieces in FORWARD],
             [[vm((32, 2 * len(p), 128), F32) for p in pieces] for pieces in FORWARD],
-            vm((512, 256), F32),
+            vm((256, 512), F32),
             [vm((32, 2 * len(p), 128), F32) for p in BACK],
             [vm((32, 2 * len(p), 128), F32) for p in BACK],
-            vm((256, 128), F32),
             vm((256, 128), F32),
             vm((384, 128), BF16),
             vm((128, 768), BF16),
@@ -469,7 +507,7 @@
             vm((1536, 256), BF16),
             vm((128, 768), BF16),
             vm((768, 128), BF16),
-            dma((15,)),
+            dma((16,)),
             dma((2,)), dma((2,)),
             dma((2,)), dma((2, 4)),
             dma((2, 3)), dma((2, 3)),
@@ -485,7 +523,15 @@
         by_time(key), by_time(value), by_time(filters), short_taps.transpose(2, 0, 1), bias,
         *[jnp.asarray(t) for t in tables],
     )
-    return conv.reshape(32, 8, 128).transpose(1, 0, 2).reshape(8, 4096) * query
+    return pl.pallas_call(
+        mix,
+        out_shape=jax.ShapeDtypeStruct((8, 4096), F32),
+        in_specs=[pl.BlockSpec(memory_space=pl.ANY)] * 2,
+        out_specs=pl.BlockSpec(memory_space=pl.ANY),
+        scratch_shapes=[vm((4, 8, 8, 128), F32), vm((8, 4096), F32), vm((8, 4096), F32), dma((3, 4))],
+        compiler_params=pltpu.CompilerParams(vmem_limit_bytes=56 * 1024 * 1024),
+        name="mix",
+    )(conv.reshape(8, 32, 128), query)
 
 
 def solution(mesh):

time: 38.7 us -> 37.9 us (0.979)
  other arithmetic: 1.57 us -> 0 us
  Pallas kernels: 37 us -> 37.7 us
    pallas_call x0 -> x1, Pallas kernels: none -> 1.61 us  [local(): pl.pallas_call(mix, out_shape=jax.ShapeDtypeStruct((8, 4096), F32), in_sp...]
    mul x1 -> x0, other arithmetic: 1.57 us -> none  [local(): return conv.reshape(32, 8, 128).transpose(1, 0, 2).reshape(8, 4096) * query]
    pallas_call x1, Pallas kernels: 37 us -> 36.1 us  [local(): pl.pallas_call(kernel, out_shape=jax.ShapeDtypeStruct((256, 128), F32), i...]
where the time goes in v5:
time: 37.9 us; the launch traced here: 37.7 us
  Pallas kernels  37.7 us (99%)
    pallas_call x1, Pallas kernels, local(): pl.pallas_call(kernel, out_shape=jax.ShapeDtypeStruct((256, 128), F32), i...  36.1 us
    pallas_call x1, Pallas kernels, local(): pl.pallas_call(mix, out_shape=jax.ShapeDtypeStruct((8, 4096), F32), in_sp...  1.61 us

profile of v5, /device:TPU:1, one launch (start us, length us, event | category | flops | bytes accessed | tf_op | source)
XLA Modules:
  0.0 37.7 jit_solution(3088375437082573668)
XLA Ops:
  0.0 36.1 %long_convolution.1 = f32[256,128]{1,0:T(8,128)} custom-call(f32[256,128]{1,0:T(8,128)} %bitcast.18, f32[256,128]{1,0:T(8,128)} %bitcast.19, f32[256,128]{1,0:T(8,128)} %bitcast.20, f32[3,2,4]{2,1,0:T(2,128)} %bitcast.21, f32[4]{0:T(128)} %bias_h.1, bf16[128,192]{1,0:T(8,128)(2,1)} %constant.22.clone.head_in2_h, bf16[256,384]{1,0:T(8,128)(2,1)} %constant.23.clone.head_in4_h, ...), custom_call_target="tpu_custom_call" | custom-call | tf_op jit(solution)/shard_map/long_convolution/pallas_call | solution.py:480
  36.1 1.6 %mix.1 = f32[8,4096]{1,0:T(8,128)} custom-call(f32[8,32,128]{2,1,0:T(8,128)} %bitcast.17, f32[8,4096]{1,0:T(8,128)} %query.1), custom_call_target="tpu_custom_call" | custom-call | tf_op jit(solution)/shard_map/mix/pallas_call | solution.py:526

commit v6 on v5

--- a/solution.py
+++ b/solution.py
@@ -34,7 +34,8 @@
     (((0, 0), (0, 1)), ((1, 0), (1, 1), (3, 0), (3, 1)), ((2, 0), (2, 1))),
     (((0, 1), (2, 1)), ((0, 0), (2, 0)), ((1, 0), (1, 1), (3, 0), (3, 1))),
 )
-BACK = ((0, 1), (2, 3), (4, 5, 6, 7))
+BACK = ((0, 4), (1, 5), (2, 3, 6, 7))
+BACK_START = [sum(len(q) for q in BACK[:p]) for p in range(len(BACK))]
 PLANE = sorted(
     ((a, b, e) for a in range(4) for b in range(4) for e in range(2) if (a, b, e) != (0, 0, 0)),
     key=lambda p: (-(2 - abs(2 - p[0])) - (2 - abs(2 - p[1])), p),
@@ -64,7 +65,7 @@
     cosines, sines = np.cos(phase), np.sin(phase)
     sines[0] = np.cos(np.pi * place)
     block_in = np.concatenate([cosines, sines], axis=0)
-    block_out = block_in.T * 2.0**-21
+    block_out = block_in.T.reshape(8, 32, 512)[[z for piece in BACK for z in piece]].reshape(256, 512) * 2.0**-21
     shift = np.stack([np.sin(2 * np.pi * nu / 512), np.cos(2 * np.pi * nu / 512), np.cos(2 * np.pi * nu / 512)])
     shift[2, 0] = -1.0
     shift = np.repeat(shift, 128, axis=0).T.astype(np.float32)
@@ -291,8 +292,8 @@
         if f == 0 and p == 1:
             l_hi.wait()
             l_turn.wait()
-        real = mm(head_in[0 : 32 * count, :], right[...])
-        imag = mm(head_in[32 * count : 64 * count, :], right[...])
+        both = mm(head_in[...], right[...])
+        real, imag = both[0 : 32 * count], both[32 * count : 64 * count]
         if f == 0 and p == 0:
             l_ti.wait()
         c, sn = turn[:, 0:128], turn[:, 128:256]
@@ -375,7 +376,7 @@
     l_bo.wait()
 
     def send_back(p):
-        low, count = 32 * BACK[p][0], len(BACK[p])
+        low, count = 32 * BACK_START[p], len(BACK[p])
         both = mm(block_out[low : low + 32 * count, :], right_i[...])
         for n in range(count):
             for i in range(2):
@@ -418,10 +419,10 @@
         real, imag = mixed[:, 0:128], mixed[:, 128:256]
         right = right_o.at[0 : 192 * count]
         put_split(right, jnp.concatenate([real * c - imag * sn, real * sn + imag * c], axis=0), 0)
-        low = 32 * BACK[p][0]
+        low = 32 * BACK_START[p]
         done_s[low : low + 32 * count, :] = mm(head_out[...], right[...])
-        for to in BACK[p]:
-            block = done_s.at[32 * to : 32 * to + 32]
+        for n, to in enumerate(BACK[p]):
+            block = done_s.at[low + 32 * n : low + 32 * n + 32]
 
             @pl.when(to == z)
             def _():
@@ -511,7 +512,7 @@
             dma((2,)), dma((2,)),
             dma((2,)), dma((2, 4)),
             dma((2, 3)), dma((2, 3)),
-            dma((3,)), dma((3,)),
+            dma((len(BACK),)), dma((len(BACK),)),
             dma(()), dma(()),
             pltpu.SemaphoreType.REGULAR((3,)),
         ],

time: 37.9 us -> 37.8 us (level)
  no operation moved by 1% of the time
where the time goes in v6:
time: 37.8 us; the launch traced here: 37.6 us
  Pallas kernels  37.6 us (99%)
    pallas_call x1, Pallas kernels, local(): pl.pallas_call(kernel, out_shape=jax.ShapeDtypeStruct((256, 128), F32), i...  36 us
    pallas_call x1, Pallas kernels, local(): pl.pallas_call(mix, out_shape=jax.ShapeDtypeStruct((8, 4096), F32), in_sp...  1.61 us

profile of v6, /device:TPU:1, one launch (start us, length us, event | category | flops | bytes accessed | tf_op | source)
XLA Modules:
  0.0 37.6 jit_solution(17927284103967203648)
XLA Ops:
  0.0 36.0 %long_convolution.1 = f32[256,128]{1,0:T(8,128)} custom-call(f32[256,128]{1,0:T(8,128)} %bitcast.18, f32[256,128]{1,0:T(8,128)} %bitcast.19, f32[256,128]{1,0:T(8,128)} %bitcast.20, f32[3,2,4]{2,1,0:T(2,128)} %bitcast.21, f32[4]{0:T(128)} %bias_h.1, bf16[128,192]{1,0:T(8,128)(2,1)} %constant.22.clone.head_in2_h, bf16[256,384]{1,0:T(8,128)(2,1)} %constant.23.clone.head_in4_h, ...), custom_call_target="tpu_custom_call" | custom-call | tf_op jit(solution)/shard_map/long_convolution/pallas_call | solution.py:481
  36.0 1.6 %mix.1 = f32[8,4096]{1,0:T(8,128)} custom-call(f32[8,32,128]{2,1,0:T(8,128)} %bitcast.17, f32[8,4096]{1,0:T(8,128)} %query.1), custom_call_target="tpu_custom_call" | custom-call | tf_op jit(solution)/shard_map/mix/pallas_call | solution.py:527

commit v7 on v6

--- a/solution.py
+++ b/solution.py
@@ -441,10 +441,10 @@
 
     for p in range(len(BACK)):
         finish_blocks(p)
-    total(out, done_recv).wait()
-    total(done_s.at[0:224], done_send).wait()
     for drain in drains:
         drain()
+    total(done_s.at[0:224], done_send).wait()
+    total(out, done_recv).wait()
 
 
 def mix(conv, query, out, conv_v, query_v, out_v, sem):

time: 37.8 us -> 37.7 us (level)
  no operation moved by 1% of the time
where the time goes in v7:
time: 37.7 us; the launch traced here: 37.6 us
  Pallas kernels  37.6 us (100%)
    pallas_call x1, Pallas kernels, local(): pl.pallas_call(kernel, out_shape=jax.ShapeDtypeStruct((256, 128), F32), i...  36 us
    pallas_call x1, Pallas kernels, local(): pl.pallas_call(mix, out_shape=jax.ShapeDtypeStruct((8, 4096), F32), in_sp...  1.61 us

profile of v7, /device:TPU:1, one launch (start us, length us, event | category | flops | bytes accessed | tf_op | source)
XLA Modules:
  0.0 37.6 jit_solution(11754620715486541515)
XLA Ops:
  0.0 36.0 %long_convolution.1 = f32[256,128]{1,0:T(8,128)} custom-call(f32[256,128]{1,0:T(8,128)} %bitcast.18, f32[256,128]{1,0:T(8,128)} %bitcast.19, f32[256,128]{1,0:T(8,128)} %bitcast.20, f32[3,2,4]{2,1,0:T(2,128)} %bitcast.21, f32[4]{0:T(128)} %bias_h.1, bf16[128,192]{1,0:T(8,128)(2,1)} %constant.22.clone.head_in2_h, bf16[256,384]{1,0:T(8,128)(2,1)} %constant.23.clone.head_in4_h, ...), custom_call_target="tpu_custom_call" | custom-call | tf_op jit(solution)/shard_map/long_convolution/pallas_call | solution.py:481
  36.0 1.6 %mix.1 = f32[8,4096]{1,0:T(8,128)} custom-call(f32[8,32,128]{2,1,0:T(8,128)} %bitcast.17, f32[8,4096]{1,0:T(8,128)} %query.1), custom_call_target="tpu_custom_call" | custom-call | tf_op jit(solution)/shard_map/mix/pallas_call | solution.py:527

commit v8 on v7

--- a/solution.py
+++ b/solution.py
@@ -371,9 +371,10 @@
     for f in range(2):
         for p in range(len(FORWARD[f])):
             forward(f, p)
+    for load in (l_bo, l_to, l_ho2, l_ho4):
+        load.wait()
     across(0)
     across(1)
-    l_bo.wait()
 
     def send_back(p):
         low, count = 32 * BACK_START[p], len(BACK[p])
@@ -410,10 +411,6 @@
                 low = (part - high.astype(F32)).astype(BF16)
                 for k, piece in enumerate((high, low, high)):
                     left_o[32 * n : 32 * n + 32, 256 * k + 128 * i : 256 * k + 128 * i + 128] = piece
-        if p == 0:
-            l_to.wait()
-            l_ho2.wait()
-            l_ho4.wait()
         mixed = mm(left_o[0 : 32 * count, :], tail_out[...])
         c, sn = turn[:, 0:128], turn[:, 128:256]
         real, imag = mixed[:, 0:128], mixed[:, 128:256]

time: 37.7 us -> 37.6 us (level)
  no operation moved by 1% of the time
where the time goes in v8:
time: 37.6 us; the launch traced here: 37.5 us
  Pallas kernels  37.4 us (99%)
    pallas_call x1, Pallas kernels, local(): pl.pallas_call(kernel, out_shape=jax.ShapeDtypeStruct((256, 128), F32), i...  35.8 us
    pallas_call x1, Pallas kernels, local(): pl.pallas_call(mix, out_shape=jax.ShapeDtypeStruct((8, 4096), F32), in_sp...  1.61 us

profile of v8, /device:TPU:1, one launch (start us, length us, event | category | flops | bytes accessed | tf_op | source)
XLA Modules:
  0.0 37.5 jit_solution(13310144171482987591)
XLA Ops:
  0.0 35.8 %long_convolution.1 = f32[256,128]{1,0:T(8,128)} custom-call(f32[256,128]{1,0:T(8,128)} %bitcast.18, f32[256,128]{1,0:T(8,128)} %bitcast.19, f32[256,128]{1,0:T(8,128)} %bitcast.20, f32[3,2,4]{2,1,0:T(2,128)} %bitcast.21, f32[4]{0:T(128)} %bias_h.1, bf16[128,192]{1,0:T(8,128)(2,1)} %constant.22.clone.head_in2_h, bf16[256,384]{1,0:T(8,128)(2,1)} %constant.23.clone.head_in4_h, ...), custom_call_target="tpu_custom_call" | custom-call | tf_op jit(solution)/shard_map/long_convolution/pallas_call | solution.py:478
  35.8 1.6 %mix.1 = f32[8,4096]{1,0:T(8,128)} custom-call(f32[8,32,128]{2,1,0:T(8,128)} %bitcast.17, f32[8,4096]{1,0:T(8,128)} %query.1), custom_call_target="tpu_custom_call" | custom-call | tf_op jit(solution)/shard_map/mix/pallas_call | solution.py:524
